TPU v7x, 128 devices: a whole 4x4x4 slice. The times are simulated.
128 devices in a mesh: row: 8 (over x, z_lo), col: 16 (over y, z_hi, core).
Axes of the slice: x: 4, y: 4, z: 4 (z_hi: 2, z_lo: 2; z = z_hi * 2 + z_lo), core: 2. Of those that a mesh axis runs over, the one named last changes fastest.
Arguments:
- hidden_in: bfloat16 [2048, 16384], P('col', 'row'), may hold values from -4 to 4
- segment_ids: int32 [2048], replicated, may hold values from 0 to 7, never falling along the last dimension, each value on 1 to 512 neighbouring positions
- q_weight: bfloat16 [16384, 16384], P(('row', 'col')), may hold values from -1 to 1
- k_weight: bfloat16 [16384, 1024], P(('row', 'col')), may hold values from -0.03203125 to 0.03203125
- value_weight: bfloat16 [16384, 1024], P(('row', 'col')), may hold values from -0.046875 to 0.046875
- out_weight: bfloat16 [16384, 16384], P(('row', 'col')), may hold values from -0.046875 to 0.046875
Outputs:
- mixed: bfloat16 [2048, 16384], P('col', 'row')
All inputs are finite; a program needn't handle non-finite values.
Results may differ from a plain program's by a relative error of at most 0.039.
Values may be sent and summed in bfloat16 or wider, within the bound.
A program may use at most 128 MiB of HBM per device.

v0:
```python
import math

import jax
import jax.numpy as jnp
from jax import lax
from jax.sharding import PartitionSpec as P

KEY_VALUE_HEADS = 8
HEAD_SIZE = 128


THETA = 500000.0
NEGATIVE = -1e30


def apply_rotation(vectors, token_positions):
    half_width = vectors.shape[-1] // 2
    indices = jnp.arange(half_width, dtype=jnp.float32)
    inverse = jnp.power(jnp.float32(THETA), -2.0 * indices / (2 * half_width))
    angles = token_positions.astype(jnp.float32)[:, None] * inverse[None, :]
    cosine = jnp.cos(angles)[:, None, :]
    sine_part = jnp.sin(angles)[:, None, :]
    front_half = vectors[..., :half_width]
    back_half = vectors[..., half_width:]
    return jnp.concatenate(
        [front_half * cosine - back_half * sine_part, back_half * cosine + front_half * sine_part],
        axis=-1,
    )


def repeat_heads(weight_table, copy_count):
    count_of_rows = weight_table.shape[0]
    grouped_rows = weight_table.reshape(count_of_rows, KEY_VALUE_HEADS, 1, HEAD_SIZE)
    return jnp.broadcast_to(
        grouped_rows, (count_of_rows, KEY_VALUE_HEADS, copy_count, HEAD_SIZE)
    ).reshape(count_of_rows, KEY_VALUE_HEADS * copy_count * HEAD_SIZE)


def attention_heads(
    queries, block_of_keys, block_of_values, query_positions, segments_query, segments_key
):
    scores = jnp.einsum(
        "qhd,kd->hqk", queries, block_of_keys, preferred_element_type=jnp.float32
    ) * (1.0 / math.sqrt(HEAD_SIZE))
    key_positions = jnp.arange(block_of_keys.shape[0], dtype=jnp.int32)
    allowed = (key_positions[None, :] <= query_positions[:, None]) & (
        segments_key[None, :] == segments_query[:, None]
    )
    scores = jnp.where(allowed[None], scores, NEGATIVE)
    largest = jnp.max(scores, axis=-1, keepdims=True)
    exponent = jnp.exp(scores - largest)
    denominator = jnp.sum(exponent, axis=-1, keepdims=True)
    probabilities = (exponent / denominator).astype(jnp.bfloat16)
    return jnp.einsum(
        "hqk,kd->qhd", probabilities, block_of_values, preferred_element_type=jnp.float32
    ).astype(jnp.bfloat16)


def body(hidden_in, segment_ids, q_weight, k_weight, value_weight, out_weight):
    count_of_columns = lax.axis_size("col")
    copy_count = count_of_columns // KEY_VALUE_HEADS
    row_index = lax.axis_index("row")
    token_total = hidden_in.shape[0] * count_of_columns
    query_count = token_total // lax.axis_size("row")
    relayed = (
        lax.all_to_all(q_weight, "col", split_axis=1, concat_axis=0, tiled=True),
        lax.all_to_all(
            repeat_heads(k_weight, copy_count), "col", split_axis=1, concat_axis=0, tiled=True
        ),
        lax.all_to_all(
            repeat_heads(value_weight, copy_count), "col", split_axis=1, concat_axis=0, tiled=True
        ),
        lax.all_to_all(out_weight, "col", split_axis=1, concat_axis=0, tiled=True),
    )
    q_relayed, k_relayed, v_relayed, out_relayed = relayed
    input_weights = jnp.concatenate([q_relayed, k_relayed, v_relayed], axis=1)
    width_of_queries = q_relayed.shape[1]
    partial_sums = jnp.dot(
        lax.all_gather(hidden_in, "col", axis=0, tiled=True),
        input_weights,
        preferred_element_type=jnp.float32,
    )
    query_positions = row_index * query_count + jnp.arange(query_count, dtype=jnp.int32)
    segments_query = lax.dynamic_slice_in_dim(segment_ids, row_index * query_count, query_count, 0)
    summed = lax.psum(partial_sums.astype(jnp.bfloat16), "row").astype(jnp.float32)
    own_rows = lax.dynamic_slice_in_dim(summed, row_index * query_count, query_count, 0)
    key_positions = jnp.arange(token_total, dtype=jnp.int32)
    block_of_keys = apply_rotation(
        summed[:, width_of_queries : width_of_queries + HEAD_SIZE][:, None, :], key_positions
    )[:, 0, :].astype(jnp.bfloat16)
    block_of_values = summed[:, width_of_queries + HEAD_SIZE :].astype(jnp.bfloat16)
    queries = apply_rotation(
        own_rows[:, :width_of_queries].reshape(
            query_count, width_of_queries // HEAD_SIZE, HEAD_SIZE
        ),
        query_positions,
    ).astype(jnp.bfloat16)
    attended = attention_heads(
        queries, block_of_keys, block_of_values, query_positions, segments_query, segment_ids
    )
    attended = attended.reshape(query_count, width_of_queries)
    head_terms = lax.dot_general(
        lax.all_gather(attended, "row", axis=0, tiled=True),
        out_relayed,
        (((1,), (1,)), ((), ())),
        preferred_element_type=jnp.float32,
    )
    return lax.psum_scatter(head_terms.astype(jnp.bfloat16), "col", scatter_dimension=0, tiled=True)


def solution(mesh):
    placed = (
        P("col", "row"),
        P(),
        P(("row", "col"), None),
        P(("row", "col"), None),
        P(("row", "col"), None),
        P(("row", "col"), None),
    )
    return jax.shard_map(
        body, mesh=mesh, in_specs=placed, out_specs=P("col", "row"), check_vma=False
    )
```

profile of v0, /device:TPU:0, one launch (start us, length us, event | category | flops | bytes accessed | tf_op | source)
XLA Modules:
  0.0 669.9 jit_solution(5759103113082365300)
XLA Ops:
  6.5 0.0 copy-start
  6.5 0.0 all-gather.3.cloned.1.call-start
  6.5 0.7 all-gather.3.cloned.1.call-update
  7.3 0.2 copy-done
  7.5 0.9 broadcast_in_dim.19
  8.4 8.0 %all-to-all-start.1 = ((bf16[128,16,128]{2,0,1:T(8,128)(2,1)}), bf16[128,16,128]{2,0,1:T(8,128)(2,1)S(1)}, u32[]{:S(2)}, u32[]{:S(2)}) async-start(bf16[128,16,128]{2,0,1:T(8,128)(2,1)} %bitcast.3), calls=%async_computation.1 | async-start | bytes 1048576 | tf_op jit(solution)/shard_map/all_to_all | solution.py:67
  16.4 0.0 copy-start.3
  16.4 6.5 copy.19
  22.9 5.9 all-to-all-done.1
  28.8 4.5 all-to-all-start
  33.3 0.0 copy-done.3
  33.4 70.7 %all-to-all-done = bf16[128,16,1024]{0,2,1:T(8,128)(2,1)} async-done(((bf16[128,16,1024]{0,2,1:T(8,128)(2,1)}), bf16[128,16,1024]{0,2,1:T(8,128)(2,1)}, u32[]{:S(2)}, u32[]{:S(2)}) %all-to-all-start) | async-done | bytes 4194336 | tf_op jit(solution)/shard_map/all_to_all | solution.py:66
  104.1 0.9 broadcast_in_dim.21
  105.0 7.5 %all-to-all-start.2 = ((bf16[128,16,128]{2,0,1:T(8,128)(2,1)}), bf16[128,16,128]{2,0,1:T(8,128)(2,1)S(1)}, u32[]{:S(2)}, u32[]{:S(2)}) async-start(bf16[128,16,128]{2,0,1:T(8,128)(2,1)} %bitcast.6), calls=%async_computation.2 | async-start | bytes 1048576 | tf_op jit(solution)/shard_map/all_to_all | solution.py:70
  112.5 0.0 all-reduce.2.cloned.1.call-start
  112.5 6.5 copy.20
  119.0 6.9 %all-to-all-done.2 = bf16[128,16,128]{2,0,1:T(8,128)(2,1)S(1)} async-done(((bf16[128,16,128]{2,0,1:T(8,128)(2,1)}), bf16[128,16,128]{2,0,1:T(8,128)(2,1)S(1)}, u32[]{:S(2)}, u32[]{:S(2)}) %all-to-all-start.2) | async-done | bytes 524320 | tf_op jit(solution)/shard_map/all_to_all | solution.py:70
  125.9 0.0 all-gather.3.cloned.1.call-done
  125.9 0.0 copy-start.4
  125.9 16.4 %fusion.6 = bf16[2048,1280]{0,1:T(8,128)(2,1)} fusion(bf16[2048,2048]{1,0:T(8,128)(2,1)} %all-gather.3.cloned.1.call-done, bf16[2048,128]{1,0:T(8,128)(2,1)S(1)} %bitcast.61, bf16[2048,128]{1,0:T(8,128)(2,1)S(1)} %bitcast.60, bf16[2048,1024]{1,0:T(8,128)(2,1)} %bitcast.58), kind=kOutput, calls=%fused_computation.11 | convolution fusion | flops 10755768320 | bytes 18874368 | tf_op jit(solution)/shard_map/dot_general | solution.py:78
  142.3 0.0 all-reduce.2.cloned.1.call-update
  142.4 0.2 all-gather.5.cloned.1.call-start
  142.6 0.0 copy-done.4
  142.6 0.1 dynamic_slice.6
  142.7 1.2 multiply_cosine_fusion.1
  143.9 1.3 fusion.12
  145.2 217.4 %all-reduce.2.cloned.1.call-done = bf16[2048,1280]{0,1:T(8,128)(2,1)} async-done(((bf16[2048,1280]{0,1:T(8,128)(2,1)}), bf16[2048,1280]{0,1:T(8,128)(2,1)}) %all-reduce.2.cloned.1.call-update) | async-done | bytes 5242896 | tf_op jit(solution)/shard_map/psum | solution.py:85
  362.6 3.9 convert_element_type.49
  366.5 0.1 constant_dynamic-slice_fusion
  366.6 0.1 slice_bitcast_fusion
  366.7 0.9 fusion.33
  367.6 0.3 copy.32
  368.0 1.4 copy.33
  369.3 2.3 fusion.19
  371.6 1.2 subtract_convert_fusion
  372.8 0.0 copy-start.2
  372.8 8.2 %fusion.22 = f32[2048,256,8]{1,0,2:T(8,128)} fusion(bf16[2048,1,64]{0,2,1:T(8,128)(2,1)S(1)} %get-tuple-element.8, bf16[2048,1,64]{0,2,1:T(8,128)(2,1)S(1)} %get-tuple-element.7, bf16[256,8,64]{2,0,1:T(8,128)(2,1)S(1)} %get-tuple-element.6, bf16[256,8,64]{2,0,1:T(8,128)(2,1)S(1)} %get-tuple-element.5), kind=kOutput, calls=%fused_computation.35 | convolution fusion | flops 1075838976 | bytes 17825792 | tf_op jit(solution)/shard_map/qhd,kd->hqk/dot_general | solution.py:42
  381.0 0.0 copy-done.2
  381.0 17.8 %fusion.34 = (f32[8,256]{1,0:T(8,128)S(1)}, f32[8,256,2048]{1,2,0:T(8,128)}) fusion(f32[2048,256,8]{1,0,2:T(8,128)} %fusion.22, pred[256,2048]{0,1:T(8,128)(4,1)S(1)} %copy-done.2), kind=kOutput, calls=%fused_computation.55 | output fusion | flops 25167872 | bytes 34086912 | tf_op jit(solution)/shard_map/sub | solution.py:51
  398.8 8.0 %fusion.13 = bf16[128,8,256]{2,0,1:T(8,128)(2,1)} fusion(f32[8,256,2048]{1,2,0:T(8,128)} %get-tuple-element.14, f32[8,256]{1,0:T(8,128)S(1)} %get-tuple-element.13, bf16[2048,1280]{0,1:T(8,128)(2,1)} %all-reduce.2.cloned.1.call-done), kind=kOutput, calls=%fused_computation.19 | convolution fusion | flops 1082392576 | bytes 17833984 | tf_op jit(solution)/shard_map/hqk,kd->qhd/dot_general | solution.py:54
  406.8 0.0 all-gather.5.cloned.1.call-update
  406.9 0.0 reduce-scatter.2.cloned.1.call-start
  406.9 6.4 copy.27
  413.3 74.2 %all_to_all.76 = bf16[128,16,1024]{0,2,1:T(8,128)(2,1)} all-to-all(bf16[128,16,1024]{0,2,1:T(8,128)(2,1)} %bitcast.56), channel_id=1, replica_groups=mesh['row'=8,'col'=16] {'col'}, dimensions={1} | all-to-all | bytes 8388608 | tf_op jit(solution)/shard_map/all_to_all | solution.py:73
  487.5 6.4 copy.28
  493.9 52.8 %all-gather.5.cloned.1.call-done = bf16[2048,1024]{0,1:T(8,128)(2,1)} async-done(((bf16[256,1024]{0,1:T(8,128)(2,1)}), bf16[2048,1024]{0,1:T(8,128)(2,1)}) %all-gather.5.cloned.1.call-update) | async-done | bytes 4194320 | tf_op jit(solution)/shard_map/all_gather | solution.py:103
  546.7 0.0 copy-start.1
  546.7 14.2 %convolution_convert_fusion = bf16[2048,2048]{1,0:T(8,128)(2,1)} fusion(bf16[2048,1024]{0,1:T(8,128)(2,1)} %all-gather.5.cloned.1.call-done, bf16[2048,1024]{1,0:T(8,128)(2,1)} %bitcast.59), kind=kOutput, calls=%fused_computation.9 | convolution fusion | flops 8594128896 | bytes 16777216 | tf_op jit(solution)/shard_map/dot_general | solution.py:102
  560.8 0.0 reduce-scatter.2.cloned.1.call-update
  560.9 102.5 %reduce-scatter.2.cloned.1.call-done = bf16[128,2048]{1,0:T(8,128)(2,1)} async-done(((bf16[2048,2048]{1,0:T(8,128)(2,1)}), bf16[128,2048]{1,0:T(8,128)(2,1)}) %reduce-scatter.2.cloned.1.call-update) | async-done | bytes 524304 | tf_op jit(solution)/shard_map/reduce_scatter | solution.py:108
  663.4 0.0 copy-done.1
  (5 shorter events, 0.1 us)
Async XLA Ops:
  6.5 1.0 copy-start
  6.5 119.4 %all-gather.3.cloned.1.call-start = ((), (), s32[]{:S(2)}) async-start(), calls=%async_computation.5 | async-start | bytes 8912896 | tf_op jit(solution)/shard_map/all_gather | solution.py:79
  8.4 20.3 %all-to-all-start.1 = ((bf16[128,16,128]{2,0,1:T(8,128)(2,1)}), bf16[128,16,128]{2,0,1:T(8,128)(2,1)S(1)}, u32[]{:S(2)}, u32[]{:S(2)}) async-start(bf16[128,16,128]{2,0,1:T(8,128)(2,1)} %bitcast.3), calls=%async_computation.1 | async-start | bytes 1048576 | tf_op jit(solution)/shard_map/all_to_all | solution.py:67
  16.4 16.9 %copy-start.3 = (bf16[128,1024]{1,0:T(8,128)(2,1)S(1)}, bf16[128,1024]{1,0:T(8,128)(2,1)}, u32[]{:S(2)}) copy-start(bf16[128,1024]{1,0:T(8,128)(2,1)} %param.10) | copy-start | bytes 786436
  28.8 75.3 %all-to-all-start = ((bf16[128,16,1024]{0,2,1:T(8,128)(2,1)}), bf16[128,16,1024]{0,2,1:T(8,128)(2,1)}, u32[]{:S(2)}, u32[]{:S(2)}) async-start(bf16[128,16,1024]{0,2,1:T(8,128)(2,1)} %bitcast.54), calls=%async_computation | async-start | bytes 8388608 | tf_op jit(solution)/shard_map/all_to_all | solution.py:66
  105.0 20.9 %all-to-all-start.2 = ((bf16[128,16,128]{2,0,1:T(8,128)(2,1)}), bf16[128,16,128]{2,0,1:T(8,128)(2,1)S(1)}, u32[]{:S(2)}, u32[]{:S(2)}) async-start(bf16[128,16,128]{2,0,1:T(8,128)(2,1)} %bitcast.6), calls=%async_computation.2 | async-start | bytes 1048576 | tf_op jit(solution)/shard_map/all_to_all | solution.py:70
  112.5 250.1 %all-reduce.2.cloned.1.call-start = ((), (), s32[]{:S(2)}) async-start(), calls=%async_computation.6 | async-start | bytes 10485760 | tf_op jit(solution)/shard_map/psum | solution.py:85
  125.9 16.7 %copy-start.4 = (s32[2048]{0:T(1024)S(1)}, s32[2048]{0:T(1024)}, u32[]{:S(2)}) copy-start(s32[2048]{0:T(1024)} %param.7) | copy-start | bytes 24580
  142.4 404.3 %all-gather.5.cloned.1.call-start = ((), (), s32[]{:S(2)}) async-start(), calls=%async_computation.7 | async-start | bytes 4718592 | tf_op jit(solution)/shard_map/all_gather | solution.py:103
  372.8 8.2 %copy-start.2 = (pred[256,2048]{0,1:T(8,128)(4,1)S(1)}, pred[256,2048]{0,1:T(8,128)(4,1)}, u32[]{:S(2)}) copy-start(pred[256,2048]{0,1:T(8,128)(4,1)} %fusion.12) | copy-start | bytes 1572868
  406.9 256.5 %reduce-scatter.2.cloned.1.call-start = ((), (), s32[]{:S(2)}) async-start(), calls=%async_computation.8 | async-start | bytes 8912896 | tf_op jit(solution)/shard_map/reduce_scatter | solution.py:108
  546.7 116.7 %copy-start.1 = (bf16[128,1024]{1,0:T(8,128)(2,1)S(1)}, bf16[128,1024]{1,0:T(8,128)(2,1)}, u32[]{:S(2)}) copy-start(bf16[128,1024]{1,0:T(8,128)(2,1)} %param.9) | copy-start | bytes 786436
Sparse Core Ops, SparseCore 0:
  9.8 108.1 all-gather.2
  142.5 220.0 all-reduce.1
  407.0 139.6 all-gather.4
  561.0 102.3 reduce-scatter.1
where the time goes:
time: 671 us; the launch traced here: 670 us
  waiting for transfers between devices  457 us (68%)
  blocking collectives  74.2 us (11%)
  matrix products  46.8 us (7%)
  local copies, waits for them, and re-layouts  30.8 us (5%)
  other arithmetic  27.6 us (4%)
  starting transfers between devices  20.3 us (3%)
  between operations  13.3 us (2%)
    psum x1, waiting for transfers between devices, body(): lax.psum(partial_sums.astype(jnp.bfloat16), 'row').astype(jnp.float32)  217 us
    reduce_scatter x1, waiting for transfers between devices, body(): lax.psum_scatter(head_terms.astype(jnp.bfloat16), 'col', scatter_dimensio...  103 us
    all_to_all x1, blocking collectives, body(): lax.all_to_all(out_weight, 'col', split_axis=1, concat_axis=0, tiled=True)  74.2 us
    all_to_all x1, waiting for transfers between devices, body(): lax.all_to_all(q_weight, 'col', split_axis=1, concat_axis=0, tiled=True)  70.7 us
    all_gather x1, waiting for transfers between devices, body(): lax.all_gather(attended, 'row', axis=0, tiled=True)  52.8 us
    sub x1, other arithmetic, attention_heads(): exponent = jnp.exp(scores - largest)  17.8 us
    dot_general x1, matrix products, body(): jnp.dot(lax.all_gather(hidden_in, 'col', axis=0, tiled=True), input_weigh...  16.4 us
    unnamed x14, local copies, waits for them, and re-layouts  14.9 us
  transfers between devices with their start and end apart: 7, of which 6 were waited for; matrix products, arithmetic and copies ran while one was open for 5% of the time, Pallas kernels for 0%

commit v1 on v0

v1 whole, which is shorter than its diff:
```python
import math

import jax
import jax.numpy as jnp
import numpy as np
from jax import lax
from jax.experimental import pallas as pl
from jax.experimental.pallas import tpu as pltpu
from jax.sharding import PartitionSpec as P

HEAD = 128
BLOCK = 128
THETA = 500000.0
NEGATIVE = -1e30
SEMAPHORES = 300
WINDOW = 5
F32 = jnp.float32
BF16 = jnp.bfloat16
MESH = pl.DeviceIdType.MESH


class Place:
    def __init__(self):
        row, col = lax.axis_index("row"), lax.axis_index("col")
        self.x, self.zl = lax.div(row, 2), lax.rem(row, 2)
        self.y, self.zh, self.c = lax.div(col, 4), lax.rem(lax.div(col, 2), 2), lax.rem(col, 2)
        self.col = col
        self.oc = 1 - self.c
        x, y, zl, zh = self.x, self.y, self.zl, self.zh
        self.ya, self.yb = y + 1 - 2 * lax.rem(y, 2), 3 - y
        self.yab = 3 - self.ya
        self.xa, self.xb = x + 1 - 2 * lax.rem(x, 2), 3 - x
        self.bits = (lax.div(x, 2), lax.rem(x + lax.div(x, 2), 2), zh, lax.rem(zl + zh, 2))
        self.partners = (
            self.dev(x=self.xb),
            self.dev(x=self.xa),
            self.dev(zh=1 - zh, zl=1 - zl),
            self.dev(zl=1 - zl),
        )
        self.token_block = (
            8 * self.bits[0] + 4 * self.bits[1] + 2 * self.bits[2] + self.bits[3]
        )

    def dev(self, **k):
        g = lambda n: k.get(n, getattr(self, n))
        return (2 * g("x") + g("zl"), 4 * g("y") + 2 * g("zh") + g("c"))

    def ycore_partners(self):
        return [
            self.dev(c=self.oc),
            self.dev(y=self.ya),
            self.dev(y=self.ya, c=self.oc),
            self.dev(y=self.yb),
            self.dev(y=self.yb, c=self.oc),
        ]

    def block_dev(self, t):
        t = lax.rem(t + 16, 16)
        n0, n1 = lax.div(t, 8), lax.rem(lax.div(t, 4), 2)
        n2, n3 = lax.rem(lax.div(t, 2), 2), lax.rem(t, 2)
        return self.dev(x=2 * n0 + lax.rem(n0 + n1, 2), zh=n2, zl=lax.rem(n2 + n3, 2))

    def all_partners(self):
        window = [self.block_dev(self.token_block + d) for i in range(1, WINDOW) for d in (i, -i)]
        return (
            self.ycore_partners() + [self.dev(zh=1 - self.zh)] + list(self.partners) + window
        )


def order(s):
    return [(s + k) % 4 for k in range(4)]


def barrier(devices):
    sem = pltpu.get_barrier_semaphore()
    for d in devices:
        pl.semaphore_signal(sem, inc=1, device_id=d, device_id_type=MESH)
    pl.semaphore_wait(sem, len(devices))


class Net:
    def __init__(self, send, recv):
        self.send, self.recv, self.n, self.open = send, recv, 0, []

    def remote(self, src, dst, dev):
        i = self.n
        self.n += 1
        cp = pltpu.make_async_remote_copy(
            src, dst, self.send.at[i], self.recv.at[i], device_id=dev, device_id_type=MESH
        )
        cp.start()
        self.open.append(cp)
        return cp

    def local(self, src, dst):
        i = self.n
        self.n += 1
        cp = pltpu.make_async_copy(src, dst, self.recv.at[i])
        cp.start()
        return cp

    def finish(self):
        for cp in self.open:
            cp.wait_send()
        self.open = []


def rows(i, n=1):
    return pl.ds(pl.multiple_of(i * BLOCK, BLOCK), n * BLOCK)


class Relay:
    def __init__(self, net, p, src, dst, rel):
        self.net, self.p, self.dst, self.rel = net, p, dst, rel
        y, c, oc = p.y, p.c, p.oc
        mine = dst.at[rows(2 * y + c)]
        self.ra = net.remote(src(2 * p.yab + c), rel.at[0], p.dev(y=p.ya))
        self.rb = net.remote(src(2 * p.yab + oc), rel.at[1], p.dev(y=p.yb))
        self.waits = [
            net.remote(src(2 * p.ya + c), mine, p.dev(y=p.ya)),
            net.remote(src(2 * p.yb + c), mine, p.dev(y=p.yb)),
            net.remote(src(2 * p.ya + oc), mine, p.dev(y=p.ya, c=oc)),
            net.remote(src(2 * p.yb + oc), mine, p.dev(y=p.yb, c=oc)),
            net.remote(src(2 * y + oc), mine, p.dev(c=oc)),
        ]
        self.own = net.local(src(2 * y + c), mine)

    def forward(self):
        p, net = self.p, self.net
        self.ra.wait_recv()
        self.waits.append(
            net.remote(self.rel.at[0], self.dst.at[rows(2 * p.ya + p.c)], p.dev(y=p.yb))
        )
        self.rb.wait_recv()
        self.waits.append(
            net.remote(
                self.rel.at[1], self.dst.at[rows(2 * p.yb + p.c)], p.dev(y=p.ya, c=p.oc)
            )
        )

    def wait(self):
        self.own.wait()
        for cp in self.waits:
            cp.wait_recv()


def prefix(bits, o, k):
    total = 0
    for i in range(k):
        total = total + bits[o[i]] * (8 >> i)
    return total


def tables():
    inverse = np.power(np.float32(THETA), -2.0 * np.arange(64, dtype=np.float32) / HEAD)
    angles = np.arange(2048, dtype=np.float32)[:, None] * inverse.astype(np.float32)[None, :]
    angles = angles.astype(np.float64)
    cos, sin = np.cos(angles), np.sin(angles)
    cos = np.concatenate([cos, cos], axis=1).astype(np.float32)
    sin = np.concatenate([-sin, sin], axis=1).astype(np.float32)
    return cos, sin


def kernel(
    h_ref, seg_ref, cos_ref, sin_ref, q_ref, k_ref, v_ref, o_ref,
    out_ref,
    hx, xs, wkv, wq, relkv, relq, part, r0, r1, r2, r3, cos, sin, kv, bias,
    att, wo, relo, acc, po, rc, ry1, ry2, fin, send, recv,
):
    p = Place()
    net = Net(send, recv)
    recvs = (r0, r1, r2, r3)
    for z in range(2):
        for yy in range(4):
            hx[z, :, yy * 256 : (yy + 1) * 256] = h_ref[
                :, yy * 512 + z * 256 : yy * 512 + z * 256 + 256
            ]
    xs[rows(p.col)] = hx[p.zh]
    barrier(p.all_partners())

    def columns(ref, width, j=0, chunk=None):
        chunk = chunk or width
        return lambda d: ref.at[:, pl.ds(pl.multiple_of(d * width + j * chunk, chunk), chunk)]

    weights = {}

    def start_weights(t):
        if t == 0:
            weights[t] = [
                Relay(net, p, columns(k_ref, HEAD), wkv.at[0], relkv.at[0]),
                Relay(net, p, columns(v_ref, HEAD), wkv.at[1], relkv.at[1]),
            ]
        elif t < 5:
            j = t - 1
            weights[t] = [Relay(net, p, columns(q_ref, 2048, j, 512), wq.at[j], relq.at[j])]
        else:
            j = t - 5
            weights[t] = [Relay(net, p, columns(o_ref, 2048, j, 512), wo.at[j], relo.at[j])]

    def forward_weights(t):
        for w in weights[t]:
            w.forward()

    def wait_weights(t):
        for w in weights[t]:
            w.wait()

    def xrows(y, zh, c):
        return xs.at[rows(4 * y + 2 * zh + c)]

    def push(block, dev):
        return net.remote(block, block, dev)

    to_a, to_b, to_core = p.dev(y=p.ya), p.dev(y=p.yb), p.dev(c=p.oc)
    oz = 1 - p.zh
    swap = net.remote(hx.at[oz], xs.at[rows(p.col)], p.dev(zh=oz))
    first = xrows(p.y, p.zh, p.c)
    a1, b1, c1 = push(first, to_a), push(first, to_b), push(first, to_core)
    table_copies = [
        net.local(cos_ref.at[rows(p.token_block)], cos),
        net.local(sin_ref.at[rows(p.token_block)], sin),
    ]
    start_weights(0)
    seg_q = jnp.transpose(
        jnp.broadcast_to(seg_ref[pl.ds(p.token_block, 1), :], (BLOCK, BLOCK))
    )
    lane = lax.broadcasted_iota(jnp.int32, (BLOCK, BLOCK), 1)
    query = p.token_block * BLOCK + lax.broadcasted_iota(jnp.int32, (BLOCK, BLOCK), 0)
    for i in range(WINDOW):
        b = lax.rem(p.token_block + 16 - (WINDOW - 1) + i, 16)
        allowed = (b * BLOCK + lane <= query) & (seg_ref[pl.ds(b, 1), :] == seg_q)
        bias[:, i * BLOCK : (i + 1) * BLOCK] = jnp.where(allowed, F32(0), F32(NEGATIVE))
    core = [c1]
    a1.wait_recv()
    f1 = push(xrows(p.ya, p.zh, p.c), to_b)
    core.append(push(xrows(p.ya, p.zh, p.c), to_core))
    b1.wait_recv()
    core.append(push(xrows(p.yb, p.zh, p.c), to_core))
    swap.wait_recv()
    second = xrows(p.y, oz, p.c)
    a2, b2 = push(second, to_a), push(second, to_b)
    core.append(push(second, to_core))
    start_weights(1)
    b2.wait_recv()
    f2 = push(xrows(p.yb, oz, p.c), to_a)
    core.append(push(xrows(p.yb, oz, p.c), to_core))
    a2.wait_recv()
    core.append(push(xrows(p.ya, oz, p.c), to_core))
    forward_weights(0)
    f1.wait_recv()
    core.append(push(xrows(p.yab, p.zh, p.c), to_core))
    start_weights(2)
    f2.wait_recv()
    core.append(push(xrows(p.yab, oz, p.c), to_core))
    for cp in table_copies:
        cp.wait()
    for cp in core:
        cp.wait_recv()

    def streams(t):
        if t == 0:
            return [(16, order(0)), (17, order(2))]
        return [((t - 1) * 4 + s, order(s)) for s in range(4)]

    def place_in(o, nat):
        return 8 * nat[o[0]] + 4 * nat[o[1]] + 2 * nat[o[2]] + nat[o[3]]

    def product(t):
        def step(m, carry):
            x = xs[pl.ds(pl.multiple_of(m * 512, 512), 512), :]
            if t == 0:
                w = jnp.concatenate([wkv[0], wkv[1]], axis=1)
            else:
                w = wq[t - 1]
            y = jnp.dot(x, w, preferred_element_type=F32).astype(BF16)
            n0, n1 = lax.div(m, 2), lax.rem(m, 2)
            for i in range(4):
                nat = (n0, n1, i // 2, i % 2)
                for g, (slot, o) in enumerate(streams(t)):
                    part[slot, place_in(o, nat)] = y[
                        i * BLOCK : (i + 1) * BLOCK, g * HEAD : (g + 1) * HEAD
                    ]
            return carry

        lax.fori_loop(0, 4, step, 0)

    pending = {}

    def scatter(t, k):
        for slot, o in streams(t):
            n = 8 >> k
            at = prefix(p.bits, o, k) + (1 - p.bits[o[k]]) * n
            pending[slot, k] = net.remote(
                part.at[slot, pl.ds(at, n)], recvs[k].at[slot], p.partners[o[k]]
            )

    def rope(u):
        return u * cos[...] + pltpu.roll(u, 64, 1) * sin[...]

    def combine(t, k):
        done = []
        for slot, o in streams(t):
            pending[slot, k].wait_recv()
            n = 8 >> k
            at = prefix(p.bits, o, k + 1)
            for i in range(n):
                total = part[slot, at + i].astype(F32) + recvs[k][slot, i].astype(F32)
                if k < 3:
                    part[slot, at + i] = total.astype(BF16)
                else:
                    done.append((total if slot == 17 else rope(total)).astype(BF16))
        return done

    window = []

    def send_window(keys, values):
        kv[WINDOW - 1, 0] = keys
        kv[WINDOW - 1, 1] = values
        for d in range(1, WINDOW):
            window.append(
                net.remote(
                    kv.at[WINDOW - 1], kv.at[WINDOW - 1 - d], p.block_dev(p.token_block + d)
                )
            )

    gathers = {}

    def gather(u, i):
        for s in range(4):
            o, k = order(s), 3 - i
            blocks = att.at[4 * u + s, pl.ds(prefix(p.bits, o, k + 1), 1 << i)]
            gathers[u, i, s] = net.remote(blocks, blocks, p.partners[o[k]])

    def attention(u, heads):
        scale = 1.0 / math.sqrt(HEAD)
        keys = jnp.concatenate([kv[i, 0] for i in range(WINDOW)], axis=0)
        values = jnp.concatenate([kv[i, 1] for i in range(WINDOW)], axis=0)
        for s, q in enumerate(heads):
            scores = lax.dot_general(
                q, keys, (((1,), (1,)), ((), ())), preferred_element_type=F32
            )
            scores = scores * scale + bias[...]
            largest = jnp.max(scores, axis=-1, keepdims=True)
            exponent = jnp.exp(scores - largest)
            denominator = jnp.sum(exponent, axis=-1, keepdims=True)
            probabilities = (exponent * (1.0 / denominator)).astype(BF16)
            att[4 * u + s, prefix(p.bits, order(s), 4)] = jnp.dot(
                probabilities, values, preferred_element_type=F32
            ).astype(BF16)
        gather(u, 0)

    def attended_rows(u, m):
        n0, n1 = lax.div(m, 2), lax.rem(m, 2)
        blocks = []
        for i in range(4):
            nat = (n0, n1, i // 2, i % 2)
            blocks.append(
                jnp.concatenate(
                    [att[4 * u + s, place_in(order(s), nat)] for s in range(4)], axis=1
                )
            )
        return jnp.concatenate(blocks, axis=0)

    def out_product(u):
        def step(m, carry):
            y = lax.dot_general(
                attended_rows(u, m), wo[u], (((1,), (1,)), ((), ())),
                preferred_element_type=F32,
            )
            for n in range(4):
                at = (n, pl.ds(pl.multiple_of(m * 512, 512), 512))
                term = y[:, n * 256 : (n + 1) * 256]
                acc[at] = term if u == 0 else acc[at] + term
            return carry

        lax.fori_loop(0, 4, step, 0)

    def last_product(n):
        def step(m, carry):
            y = lax.dot_general(
                attended_rows(3, m), wo[3, n * 256 : (n + 1) * 256],
                (((1,), (1,)), ((), ())), preferred_element_type=F32,
            )
            total = (acc[n, pl.ds(pl.multiple_of(m * 512, 512), 512)] + y).astype(BF16)
            for i in range(4):
                po[n, i % 2, 2 * m + i // 2] = total[i * BLOCK : (i + 1) * BLOCK]
            return carry

        lax.fori_loop(0, 4, step, 0)

    for t in range(13):
        for u in range(4):
            i = t - (u + 5) - 1
            if 0 <= i < 4:
                for s in range(4):
                    gathers[u, i, s].wait_recv()
                if i < 3:
                    gather(u, i + 1)
        finished = []
        for u in range(5):
            k = t - u - 1
            if 0 <= k < 4:
                done = combine(u, k)
                if k < 3:
                    scatter(u, k + 1)
                elif u == 0:
                    send_window(*done)
                else:
                    finished.append((u - 1, done))
        if t + 1 < 9:
            forward_weights(t + 1)
        if t < 5:
            wait_weights(t)
            if t + 3 < 5:
                start_weights(t + 3)
            if 5 <= t + 2:
                start_weights(t + 2)
            product(t)
            scatter(t, 0)
        elif t + 2 < 9:
            start_weights(t + 2)
        if t == 5:
            for cp in window:
                cp.wait_recv()
        for u, heads in finished:
            attention(u, heads)
        u = t - 9
        if 0 <= u < 3:
            wait_weights(5 + u)
            out_product(u)
    wait_weights(8)

    y, ya, yb, yab = p.y, p.ya, p.yb, p.yab
    step1, step2, step3, step4 = {}, {}, {}, {}

    def add(n, at, other):
        po[n, p.c, at] = (po[n, p.c, at].astype(F32) + other.astype(F32)).astype(BF16)

    def sum_cores(n):
        step1[n].wait_recv()
        for i in range(8):
            add(n, i, rc[n, i])
        mine = po.at[n, p.c]
        step2[n] = [
            net.remote(mine.at[2 * yab], ry1.at[n, 0, 0], to_a),
            net.remote(mine.at[2 * yab + 1], ry1.at[n, 1, 0], to_b),
            net.remote(mine.at[2 * ya], ry1.at[n, 0, 1], to_a),
            net.remote(mine.at[2 * yb + 1], ry1.at[n, 1, 1], to_b),
        ]

    def sum_first(n):
        for cp in step2[n]:
            cp.wait_recv()
        add(n, 2 * yb, ry1[n, 0, 0])
        add(n, 2 * ya + 1, ry1[n, 1, 0])
        mine = po.at[n, p.c]
        step3[n] = [
            net.remote(mine.at[2 * yb], ry2.at[n, 0], to_b),
            net.remote(mine.at[2 * ya + 1], ry2.at[n, 1], to_a),
        ]
        add(n, 2 * y, ry1[n, 0, 1])
        add(n, 2 * y + 1, ry1[n, 1, 1])

    def sum_second(n):
        for cp in step3[n]:
            cp.wait_recv()
        add(n, 2 * y, ry2[n, 0])
        add(n, 2 * y + 1, ry2[n, 1])
        step4[n] = net.remote(
            po.at[n, p.c, 2 * y + oz], fin.at[n, p.zh], p.dev(zh=oz)
        )
        fin[n, p.zh] = po[n, p.c, 2 * y + p.zh]

    def finish(n):
        step4[n].wait_recv()
        for z in range(2):
            out_ref[:, n * 512 + z * 256 : n * 512 + z * 256 + 256] = fin[n, z]

    for n in range(8):
        if n < 4:
            last_product(n)
            step1[n] = net.remote(po.at[n, p.oc], rc.at[n], to_core)
        if 0 <= n - 3 < 4:
            sum_second(n - 3)
        if 0 <= n - 2 < 4:
            sum_first(n - 2)
        if 0 <= n - 1 < 4:
            sum_cores(n - 1)
        if 0 <= n - 4 < 4:
            finish(n - 4)
    net.finish()


def body(hidden_in, segment_ids, q_weight, k_weight, value_weight, out_weight):
    vmem = pl.BlockSpec(memory_space=pltpu.VMEM)
    hbm = pl.BlockSpec(memory_space=pl.ANY)
    cos, sin = tables()
    blocks = lambda *shape: pltpu.VMEM(shape, BF16)
    return pl.pallas_call(
        kernel,
        out_shape=jax.ShapeDtypeStruct((BLOCK, 2048), BF16),
        in_specs=[vmem, vmem, hbm, hbm, hbm, hbm, hbm, hbm],
        out_specs=vmem,
        scratch_shapes=[
            blocks(2, BLOCK, 1024),
            blocks(2048, 1024),
            blocks(2, 1024, HEAD),
            blocks(4, 1024, 512),
            blocks(2, 2, BLOCK, HEAD),
            blocks(4, 2, BLOCK, 512),
            blocks(18, 16, BLOCK, HEAD),
            blocks(18, 8, BLOCK, HEAD),
            blocks(18, 4, BLOCK, HEAD),
            blocks(18, 2, BLOCK, HEAD),
            blocks(18, 1, BLOCK, HEAD),
            pltpu.VMEM((BLOCK, HEAD), F32),
            pltpu.VMEM((BLOCK, HEAD), F32),
            blocks(WINDOW, 2, BLOCK, HEAD),
            pltpu.VMEM((BLOCK, WINDOW * BLOCK), F32),
            blocks(16, 16, BLOCK, HEAD),
            blocks(4, 1024, 512),
            blocks(4, 2, BLOCK, 512),
            pltpu.VMEM((4, 2048, 256), F32),
            blocks(4, 2, 8, BLOCK, 256),
            blocks(4, 8, BLOCK, 256),
            blocks(4, 2, 2, BLOCK, 256),
            blocks(4, 2, BLOCK, 256),
            blocks(4, 2, BLOCK, 256),
            pltpu.SemaphoreType.DMA((SEMAPHORES,)),
            pltpu.SemaphoreType.DMA((SEMAPHORES,)),
        ],
        compiler_params=pltpu.CompilerParams(
            collective_id=0, has_side_effects=True, vmem_limit_bytes=63 << 20
        ),
    )(hidden_in, segment_ids.reshape(16, BLOCK), cos, sin, q_weight, k_weight, value_weight,
      out_weight)


def solution(mesh):
    placed = (
        P("col", "row"),
        P(),
        P(("row", "col"), None),
        P(("row", "col"), None),
        P(("row", "col"), None),
        P(("row", "col"), None),
    )
    return jax.shard_map(
        body, mesh=mesh, in_specs=placed, out_specs=P("col", "row"), check_vma=False
    )
```

time: 671 us -> 207 us (0.31)
  waiting for transfers between devices: 457 us -> 0 us
  Pallas kernels: 0 us -> 205 us
  blocking collectives: 74.2 us -> 0 us
  matrix products: 46.8 us -> 0 us
  local copies, waits for them, and re-layouts: 30.8 us -> 1.88 us
  other arithmetic: 27.6 us -> 0 us
  starting transfers between devices: 20.3 us -> 0 us
  between operations: 13.3 us -> 0.01 us
    psum x1 -> x0, waiting for transfers between devices: 217 us -> none  [body(): lax.psum(partial_sums.astype(jnp.bfloat16), 'row').astype(jnp.float32)]
    pallas_call x0 -> x1, Pallas kernels: none -> 205 us  [body(): pl.pallas_call(kernel, out_shape=jax.ShapeDtypeStruct((BLOCK, 2048), BF16...]
    reduce_scatter x1 -> x0, waiting for transfers between devices: 103 us -> none  [body(): lax.psum_scatter(head_terms.astype(jnp.bfloat16), 'col', scatter_dimensio...]
    all_to_all x3 -> x0, waiting for transfers between devices: 83.5 us -> none  [the longest x1 70.7 us: body(): lax.all_to_all(q_weight, 'col', split_axis=1, concat_axis=0, tiled=True)]
    all_to_all x1 -> x0, blocking collectives: 74.2 us -> none  [body(): lax.all_to_all(out_weight, 'col', split_axis=1, concat_axis=0, tiled=True)]
    all_gather x2 -> x0, waiting for transfers between devices: 52.8 us -> none  [the longest x1 52.8 us: body(): lax.all_gather(attended, 'row', axis=0, tiled=True)]
    dot_general x4 -> x0, matrix products: 46.8 us -> none  [the longest x1 16.4 us: body(): jnp.dot(lax.all_gather(hidden_in, 'col', axis=0, tiled=True), input_weigh...]
    all_to_all x3 -> x0, starting transfers between devices: 20 us -> none  [the longest x1 7.97 us: body(): lax.all_to_all(repeat_heads(k_weight, copy_count), 'col', split_axis=1, c...]
  transfers between devices with their start and end apart: 7 -> 0, of which waited for: 6 -> 0; matrix products, arithmetic and copies ran while one was open for 5% -> 0% of each run, Pallas kernels for 0% -> 0%
where the time goes in v1:
time: 207 us
  Pallas kernels  205 us (99%)
    pallas_call x1, Pallas kernels, body(): pl.pallas_call(kernel, out_shape=jax.ShapeDtypeStruct((BLOCK, 2048), BF16...  205 us

profile of v1, /device:TPU:0, one launch (start us, length us, event | category | flops | bytes accessed | tf_op | source)
XLA Modules:
  0.0 207.1 jit_solution(1438066036805201064)
XLA Ops:
  0.0 205.2 %shard_map.82 = bf16[128,2048]{1,0:T(8,128)(2,1)} custom-call(bf16[128,2048]{1,0:T(8,128)(2,1)} %h_ref.1, s32[16,128]{1,0:T(8,128)} %bitcast.1, f32[2048,128]{1,0:T(8,128)} %constant.4.clone.cos_ref, f32[2048,128]{1,0:T(8,128)} %constant.5.clone.sin_ref, bf16[128,16384]{1,0:T(8,128)(2,1)} %q_ref.1, bf16[128,1024]{1,0:T(8,128)(2,1)} %k_ref.1, ...), custom_call_target="tpu_custom_call" | custom-call | tf_op jit(solution)/shard_map/pallas_call | solution.py:499
  205.2 1.9 copy.10

commit v2 on v1

v2 whole, which is shorter than its diff:
```python
import math

import jax
import jax.numpy as jnp
import numpy as np
from jax import lax
from jax.experimental import pallas as pl
from jax.experimental.pallas import tpu as pltpu
from jax.sharding import PartitionSpec as P

HEAD = 128
BLOCK = 128
HALF = 64
THETA = 500000.0
NEGATIVE = -1e30
SEMAPHORES = 400
WINDOW = 5
F32 = jnp.float32
BF16 = jnp.bfloat16
MESH = pl.DeviceIdType.MESH


class Place:
    def __init__(self):
        row, col = lax.axis_index("row"), lax.axis_index("col")
        self.x, self.zl = lax.div(row, 2), lax.rem(row, 2)
        self.y, self.zh, self.c = lax.div(col, 4), lax.rem(lax.div(col, 2), 2), lax.rem(col, 2)
        self.col = col
        self.oc = 1 - self.c
        x, y, zl, zh = self.x, self.y, self.zl, self.zh
        self.ya, self.yb = y + 1 - 2 * lax.rem(y, 2), 3 - y
        self.yab = 3 - self.ya
        self.xa, self.xb = x + 1 - 2 * lax.rem(x, 2), 3 - x
        self.bits = (lax.div(x, 2), lax.rem(x + lax.div(x, 2), 2), zh, lax.rem(zl + zh, 2))
        self.partners = (
            self.dev(x=self.xb),
            self.dev(x=self.xa),
            self.dev(zh=1 - zh, zl=1 - zl),
            self.dev(zl=1 - zl),
        )
        self.token_block = (
            8 * self.bits[0] + 4 * self.bits[1] + 2 * self.bits[2] + self.bits[3]
        )

    def dev(self, **k):
        g = lambda n: k.get(n, getattr(self, n))
        return (2 * g("x") + g("zl"), 4 * g("y") + 2 * g("zh") + g("c"))

    def ycore_partners(self):
        return [
            self.dev(c=self.oc),
            self.dev(y=self.ya),
            self.dev(y=self.ya, c=self.oc),
            self.dev(y=self.yb),
            self.dev(y=self.yb, c=self.oc),
        ]

    def block_dev(self, t):
        t = lax.rem(t + 16, 16)
        n0, n1 = lax.div(t, 8), lax.rem(lax.div(t, 4), 2)
        n2, n3 = lax.rem(lax.div(t, 2), 2), lax.rem(t, 2)
        return self.dev(x=2 * n0 + lax.rem(n0 + n1, 2), zh=n2, zl=lax.rem(n2 + n3, 2))

    def all_partners(self):
        window = [self.block_dev(self.token_block + d) for i in range(1, WINDOW) for d in (i, -i)]
        return (
            self.ycore_partners()
            + [self.dev(y=y, zh=1 - self.zh) for y in (self.y, self.ya, self.yb)]
            + list(self.partners)
            + window
        )


def order(s):
    return [(s + k) % 4 for k in range(4)]


def barrier(devices):
    sem = pltpu.get_barrier_semaphore()
    for d in devices:
        pl.semaphore_signal(sem, inc=1, device_id=d, device_id_type=MESH)
    pl.semaphore_wait(sem, len(devices))


class Net:
    def __init__(self, send, recv):
        self.send, self.recv, self.n, self.open = send, recv, 0, []

    def remote(self, src, dst, dev):
        i = self.n
        self.n += 1
        cp = pltpu.make_async_remote_copy(
            src, dst, self.send.at[i], self.recv.at[i], device_id=dev, device_id_type=MESH
        )
        cp.start()
        self.open.append(cp)
        return cp

    def local(self, src, dst):
        i = self.n
        self.n += 1
        cp = pltpu.make_async_copy(src, dst, self.recv.at[i])
        cp.start()
        return cp

    def finish(self):
        for cp in self.open:
            cp.wait_send()
        self.open = []


def rows(i, n=1):
    return pl.ds(pl.multiple_of(i * BLOCK, BLOCK), n * BLOCK)


class Relay:
    def __init__(self, net, p, src, dst, rel):
        self.net, self.p, self.dst, self.rel = net, p, dst, rel
        y, c, oc = p.y, p.c, p.oc
        mine = dst.at[rows(2 * y + c)]
        self.ra = net.remote(src(2 * p.yab + c), rel.at[0], p.dev(y=p.ya))
        self.rb = net.remote(src(2 * p.yab + oc), rel.at[1], p.dev(y=p.yb))
        self.waits = [
            net.remote(src(2 * p.ya + c), mine, p.dev(y=p.ya)),
            net.remote(src(2 * p.yb + c), mine, p.dev(y=p.yb)),
            net.remote(src(2 * p.ya + oc), mine, p.dev(y=p.ya, c=oc)),
            net.remote(src(2 * p.yb + oc), mine, p.dev(y=p.yb, c=oc)),
            net.remote(src(2 * y + oc), mine, p.dev(c=oc)),
        ]
        self.own = net.local(src(2 * y + c), mine)

    def forward(self, way):
        p = self.p
        (self.ra, self.rb)[way].wait_recv()
        origin = (p.ya, p.yb)[way]
        to = (p.dev(y=p.yb), p.dev(y=p.ya, c=p.oc))[way]
        self.waits.append(
            self.net.remote(self.rel.at[way], self.dst.at[rows(2 * origin + p.c)], to)
        )

    def wait(self):
        self.own.wait()
        for cp in self.waits:
            cp.wait_recv()


def prefix(bits, o, k):
    total = 0
    for i in range(k):
        total = total + bits[o[i]] * (8 >> i)
    return total


def tables():
    inverse = np.power(np.float32(THETA), -2.0 * np.arange(64, dtype=np.float32) / HEAD)
    angles = np.arange(2048, dtype=np.float32)[:, None] * inverse.astype(np.float32)[None, :]
    angles = angles.astype(np.float64)
    cos, sin = np.cos(angles), np.sin(angles)
    cos = np.concatenate([cos, cos], axis=1).astype(np.float32)
    sin = np.concatenate([-sin, sin], axis=1).astype(np.float32)
    return cos, sin


ORDER = (
    ("H","swap"), ("H","a1"), ("S",0), ("F",0,0), ("S",1), ("H","b2"), ("F",1,0),
    ("H","f1"), ("H","f2"), ("F",0,1), ("F",1,1), ("H","b1"), ("S",2), ("H","a2"), ("P",0),
    ("P",1), ("F",2,0), ("F",2,1), ("S",3), ("C",17,0), ("C",16,0), ("C",3,0), ("C",1,0),
    ("C",2,0), ("C",0,0), ("F",3,0), ("F",3,1), ("C",16,1), ("C",17,1), ("P",2), ("C",16,2),
    ("C",0,1), ("C",1,1), ("C",3,1), ("C",2,1), ("S",4), ("C",17,2), ("P",3), ("C",7,0),
    ("C",5,0), ("F",4,1), ("F",4,0), ("S",5), ("C",2,2), ("C",4,0), ("C",1,2), ("C",6,0),
    ("S",6), ("C",16,3), ("S",7), ("C",3,2), ("C",0,2), ("S",8), ("C",17,3), ("C",11,0),
    ("C",9,0), ("C",2,3), ("C",10,0), ("C",8,0), ("F",5,0), ("C",7,1), ("C",5,1), ("C",6,1),
    ("C",4,1), ("P",4), ("C",3,3), ("C",4,2), ("C",11,1), ("C",0,3), ("C",10,1), ("C",1,3),
    ("A",0), ("C",5,2), ("C",7,2), ("C",9,1), ("C",8,1), ("C",6,2), ("C",12,0), ("C",13,0),
    ("C",15,0), ("G",3,0,0), ("C",14,0), ("G",3,0,1), ("C",10,2), ("C",11,2), ("G",2,0,0),
    ("G",1,0,1), ("C",4,3), ("G",0,0,1), ("G",1,0,0), ("C",7,3), ("C",5,3), ("G",0,0,0),
    ("C",9,2), ("C",6,3), ("G",2,0,1), ("A",1), ("C",8,2), ("G",2,1,0), ("C",14,1),
    ("G",1,1,1), ("C",15,1), ("C",13,1), ("G",3,1,1), ("C",10,3), ("C",12,1), ("G",3,1,0),
    ("G",2,1,1), ("G",5,0,0), ("G",0,1,1), ("G",0,1,0), ("G",4,0,1), ("C",9,3), ("G",1,1,0),
    ("G",4,0,0), ("C",11,3), ("C",8,3), ("G",6,0,0), ("G",7,0,1), ("A",2), ("G",5,0,1),
    ("G",4,1,1), ("C",13,2), ("C",12,2), ("G",0,2,0), ("C",15,2), ("C",14,2), ("G",3,2,1),
    ("F",7,0), ("G",1,2,0), ("G",6,1,0), ("G",2,2,1), ("F",8,0), ("G",3,2,0), ("G",9,0,1),
    ("G",8,0,1), ("F",5,1), ("G",10,0,1), ("G",11,0,1), ("G",6,0,1), ("G",7,0,0),
    ("G",5,1,1), ("G",2,2,0), ("C",13,3), ("G",0,2,1), ("C",15,3), ("C",12,3), ("G",7,1,1),
    ("G",1,2,1), ("C",14,3), ("A",3), ("G",6,1,1), ("F",7,1), ("G",11,0,0), ("G",10,0,0),
    ("G",5,1,0), ("G",11,1,1), ("G",10,1,1), ("G",8,1,1), ("F",8,1), ("G",8,0,0),
    ("G",4,1,0), ("F",6,1), ("G",9,0,0), ("G",7,1,0), ("F",6,0), ("G",9,1,1), ("G",13,0,1),
    ("G",12,0,1), ("G",14,0,1), ("G",15,0,1), ("G",14,0,0), ("G",5,2,1), ("G",7,2,1),
    ("G",4,2,1), ("G",15,0,0), ("G",6,2,1), ("O",0,1), ("G",14,1,1), ("G",12,1,1),
    ("G",11,2,1), ("G",13,1,1), ("G",12,0,0), ("G",15,1,1), ("G",8,2,1), ("G",10,2,1),
    ("G",13,0,0), ("G",9,2,1), ("O",0,0), ("G",13,2,1), ("G",14,2,1), ("G",12,2,1),
    ("G",15,2,1), ("G",14,1,0), ("O",1,1), ("G",11,1,0), ("G",10,1,0), ("G",15,1,0),
    ("G",8,1,0), ("G",7,2,0), ("G",4,2,0), ("G",12,1,0), ("G",9,1,0), ("G",13,1,0),
    ("O",2,1), ("G",5,2,0), ("G",6,2,0), ("L",1,0), ("G",9,2,0), ("L",1,1), ("G",10,2,0),
    ("G",11,2,0), ("G",14,2,0), ("G",8,2,0), ("G",13,2,0), ("G",12,2,0), ("G",15,2,0),
    ("U",0,1,0), ("O",1,0), ("U",0,1,1), ("O",2,0), ("U",1,1,0), ("L",0,1), ("L",0,0),
    ("U",1,1,1), ("U",0,0,1), ("U",0,0,0), ("U",1,0,1), ("U",2,1,1), ("U",1,0,0),
    ("U",2,1,0), ("U",2,0,1), ("U",2,0,0),
)


def kernel(
    h_ref, seg_ref, cos_ref, sin_ref, q_ref, k_ref, v_ref, o_ref,
    out_ref,
    hx, xs, wkv, wq, relkv, relq, part, r0, r1, r2, r3, cos, sin, kv, bias,
    att, wo, relo, acc, po, rc, ry1, ry2, fin, send, recv,
):
    p = Place()
    net = Net(send, recv)
    recvs = (r0, r1, r2, r3)
    for z in range(2):
        for yy in range(4):
            hx[z, :, yy * 256 : (yy + 1) * 256] = h_ref[
                :, yy * 512 + z * 256 : yy * 512 + z * 256 + 256
            ]
    xs[rows(p.col)] = hx[p.zh]
    barrier(p.all_partners())

    flying = {}

    def arrive(*keys):
        for key in keys:
            flying.pop(key).wait_recv()

    def arrive_once(*keys):
        arrive(*[key for key in keys if key in flying])

    to_a, to_b, to_core = p.dev(y=p.ya), p.dev(y=p.yb), p.dev(c=p.oc)
    oz = 1 - p.zh

    def push(key, y, zh, dev):
        block = xs.at[rows(4 * y + 2 * zh + p.c)]
        flying[key] = net.remote(block, block, dev)

    def swap(key, y):
        flying[key] = net.remote(hx.at[oz], xs.at[rows(p.col)], p.dev(y=y, zh=oz))

    swap("swap", p.y)
    push("a1", p.y, p.zh, to_a)
    push("b1", p.y, p.zh, to_b)
    push("c1", p.y, p.zh, to_core)
    swap("a2", p.ya)
    swap("b2", p.yb)
    table_copies = [
        net.local(cos_ref.at[rows(p.token_block)], cos),
        net.local(sin_ref.at[rows(p.token_block)], sin),
    ]

    def act_h(name):
        arrive(name)
        if name == "a1":
            push("f1", p.ya, p.zh, to_b)
            push("h1", p.ya, p.zh, to_core)
        elif name == "b1":
            push("h2", p.yb, p.zh, to_core)
        elif name == "swap":
            push("c2", p.y, oz, to_core)
        elif name == "b2":
            push("f2", p.yb, oz, to_a)
            push("h3", p.yb, oz, to_core)
        elif name == "a2":
            push("h4", p.ya, oz, to_core)
        elif name == "f1":
            push("h5", p.yab, p.zh, to_core)
        elif name == "f2":
            push("h6", p.yab, oz, to_core)

    def columns(ref, width, j=0, chunk=None):
        chunk = chunk or width
        return lambda d: ref.at[:, pl.ds(pl.multiple_of(d * width + j * chunk, chunk), chunk)]

    weights = {}

    def act_s(t):
        if t == 0:
            weights[t] = [
                Relay(net, p, columns(k_ref, HEAD), wkv.at[0], relkv.at[0]),
                Relay(net, p, columns(v_ref, HEAD), wkv.at[1], relkv.at[1]),
            ]
        elif t < 5:
            j = t - 1
            weights[t] = [Relay(net, p, columns(q_ref, 2048, j, 512), wq.at[j], relq.at[j])]
        else:
            j = t - 5
            weights[t] = [Relay(net, p, columns(o_ref, 2048, j, 512), wo.at[j], relo.at[j])]

    def act_f(t, way):
        for w in weights[t]:
            w.forward(way)

    def wait_weights(t):
        for w in weights.pop(t, ()):
            w.wait()

    def slot_order(slot):
        return order((0, 2)[slot - 16] if slot >= 16 else slot % 4)

    def place_in(o, nat):
        return 8 * nat[o[0]] + 4 * nat[o[1]] + 2 * nat[o[2]] + nat[o[3]]

    def scatter(slot, k):
        o, n = slot_order(slot), 8 >> k
        at = prefix(p.bits, o, k) + (1 - p.bits[o[k]]) * n
        flying["r", slot, k] = net.remote(
            part.at[slot, pl.ds(at, n)], recvs[k].at[slot], p.partners[o[k]]
        )

    def act_p(t):
        arrive_once("c1", "c2", "h1", "h2", "h3", "h4", "h5", "h6")
        wait_weights(t)
        slots = (16, 17) if t == 0 else range(4 * t - 4, 4 * t)

        def step(m, carry):
            x = xs[pl.ds(pl.multiple_of(m * 512, 512), 512), :]
            if t == 0:
                w = jnp.concatenate([wkv[0], wkv[1]], axis=1)
            else:
                w = wq[t - 1]
            y = jnp.dot(x, w, preferred_element_type=F32).astype(BF16)
            n0, n1 = lax.div(m, 2), lax.rem(m, 2)
            for i in range(4):
                nat = (n0, n1, i // 2, i % 2)
                for g, slot in enumerate(slots):
                    part[slot, place_in(slot_order(slot), nat)] = y[
                        i * BLOCK : (i + 1) * BLOCK, g * HEAD : (g + 1) * HEAD
                    ]
            return carry

        lax.fori_loop(0, 4, step, 0)
        for slot in slots:
            scatter(slot, 0)

    def rope(u):
        while table_copies:
            table_copies.pop().wait()
        return u * cos[...] + pltpu.roll(u, 64, 1) * sin[...]

    queries = {}

    def act_c(slot, k):
        arrive(("r", slot, k))
        o, n = slot_order(slot), 8 >> k
        at = prefix(p.bits, o, k + 1)
        if k < 3:
            for i in range(n):
                part[slot, at + i] = part[slot, at + i] + recvs[k][slot, i]
            scatter(slot, k + 1)
            return
        total = part[slot, at].astype(F32) + recvs[k][slot, 0].astype(F32)
        if slot < 16:
            queries[slot] = (rope(total) * (math.log2(math.e) / math.sqrt(HEAD))).astype(BF16)
        else:
            which = slot - 16
            kv[which, WINDOW - 1] = (total if which else rope(total)).astype(BF16)
            for d in range(1, WINDOW):
                flying["window", which, d] = net.remote(
                    kv.at[which, WINDOW - 1],
                    kv.at[which, WINDOW - 1 - d],
                    p.block_dev(p.token_block + d),
                )

    def gather(slot, i, half):
        o, k = slot_order(slot), 3 - i
        blocks = att.at[half, slot, pl.ds(prefix(p.bits, o, k + 1), 1 << i)]
        flying["g", slot, i, half] = net.remote(blocks, blocks, p.partners[o[k]])

    def act_a(u):
        arrive_once(*[("window", which, d) for which in range(2) for d in range(1, WINDOW)])
        slots = range(4 * u, 4 * u + 4)
        scores = lax.dot_general(
            jnp.concatenate([queries.pop(slot) for slot in slots], axis=0),
            kv[0].reshape(WINDOW * BLOCK, HEAD),
            (((1,), (1,)), ((), ())),
            preferred_element_type=F32,
        )
        scores = scores.reshape(4, BLOCK, WINDOW * BLOCK) + bias[...][None]
        scores = scores.reshape(4 * BLOCK, WINDOW * BLOCK)
        exponent = jnp.exp2(scores - jnp.max(scores, axis=-1, keepdims=True))
        denominator = jnp.sum(exponent, axis=-1, keepdims=True)
        attended = jnp.dot(
            exponent.astype(BF16),
            kv[1].reshape(WINDOW * BLOCK, HEAD),
            preferred_element_type=F32,
        )
        attended = (attended * (1.0 / denominator)).astype(BF16)
        for s, slot in enumerate(slots):
            at = prefix(p.bits, order(s), 4)
            for half in range(2):
                low = s * BLOCK + half * HALF
                att[half, slot, at] = attended[low : low + HALF]
                gather(slot, 0, half)

    def act_g(slot, i, half):
        arrive(("g", slot, i, half))
        gather(slot, i + 1, half)

    def attended_rows(u, half, m):
        blocks = []
        for i in range(8):
            nat = (m, i // 4, i // 2 % 2, i % 2)
            blocks.append(
                jnp.concatenate(
                    [att[half, 4 * u + s, place_in(order(s), nat)] for s in range(4)], axis=1
                )
            )
        return jnp.concatenate(blocks, axis=0)

    def act_o(u, half):
        wait_weights(5 + u)
        arrive(*[("g", 4 * u + s, 3, half) for s in range(4)])

        def step(m, carry):
            y = lax.dot_general(
                attended_rows(u, half, m), wo[u], (((1,), (1,)), ((), ())),
                preferred_element_type=F32,
            )
            for f in range(2):
                at = (half, f, pl.ds(pl.multiple_of(m * 512, 512), 512))
                term = y[:, f * 512 : (f + 1) * 512]
                acc[at] = term if u == 0 else acc[at] + term
            return carry

        lax.fori_loop(0, 2, step, 0)

    y, ya, yb, yab = p.y, p.ya, p.yb, p.yab

    def act_l(half, f):
        wait_weights(8)
        arrive_once(*[("g", 12 + s, 3, half) for s in range(4)])

        def step(m, carry):
            term = lax.dot_general(
                attended_rows(3, half, m), wo[3, f * 512 : (f + 1) * 512],
                (((1,), (1,)), ((), ())), preferred_element_type=F32,
            )
            total = acc[half, f, pl.ds(pl.multiple_of(m * 512, 512), 512)] + term
            total = total.astype(BF16)
            for i in range(8):
                po[half, f, i % 2, 4 * m + i // 2] = total[i * HALF : (i + 1) * HALF]
            return carry

        lax.fori_loop(0, 2, step, 0)
        flying["c", half, f] = net.remote(po.at[half, f, p.oc], rc.at[half, f], to_core)

    def act_u(stage, half, f):
        mine, key = po.at[half, f, p.c], ("u", stage, half, f)
        one, two = ry1.at[half, f], ry2.at[half, f]

        def add(at, other):
            mine[at] = mine[at] + other

        def hand(block, dst, dev):
            flying["u", stage + 1, half, f, len(flying)] = net.remote(mine.at[block], dst, dev)

        if stage == 0:
            arrive(("c", half, f))
            for i in range(8):
                add(i, rc[half, f, i])
            hand(2 * yab + p.zh, one.at[0, 0], to_a)
            hand(2 * yab + oz, one.at[1, 0], to_b)
            hand(2 * ya + p.zh, one.at[0, 1], to_a)
            hand(2 * yb + oz, one.at[1, 1], to_b)
            return
        arrive(*[k for k in flying if k[:4] == key])
        if stage == 1:
            add(2 * yb + p.zh, one[0, 0])
            hand(2 * yb + p.zh, two.at[0], to_b)
            add(2 * ya + oz, one[1, 0])
            hand(2 * ya + oz, two.at[1], p.dev(y=ya, zh=oz))
            add(2 * y + oz, one[1, 1])
            hand(2 * y + oz, two.at[2], p.dev(zh=oz))
            add(2 * y + p.zh, one[0, 1])
            return
        fin[half, f, p.zh] = mine[2 * y + p.zh] + two[0]
        fin[half, f, oz] = two[1] + two[2]
        for z in range(2):
            for e in range(2):
                at = (2 * f + e) * 512 + z * 256
                out_ref[half * HALF : (half + 1) * HALF, at : at + 256] = fin[
                    half, f, z, :, e * 256 : (e + 1) * 256
                ]

    seg_q = jnp.transpose(
        jnp.broadcast_to(seg_ref[pl.ds(p.token_block, 1), :], (BLOCK, BLOCK))
    )
    lane = lax.broadcasted_iota(jnp.int32, (BLOCK, BLOCK), 1)
    query = p.token_block * BLOCK + lax.broadcasted_iota(jnp.int32, (BLOCK, BLOCK), 0)
    for i in range(WINDOW):
        b = lax.rem(p.token_block + 16 - (WINDOW - 1) + i, 16)
        allowed = (b * BLOCK + lane <= query) & (seg_ref[pl.ds(b, 1), :] == seg_q)
        bias[:, i * BLOCK : (i + 1) * BLOCK] = jnp.where(allowed, F32(0), F32(NEGATIVE))

    actions = dict(
        H=act_h, S=act_s, F=act_f, P=act_p, C=act_c, A=act_a, G=act_g, O=act_o, L=act_l, U=act_u
    )
    for name, *arguments in ORDER:
        actions[name](*arguments)
    net.finish()


def body(hidden_in, segment_ids, q_weight, k_weight, value_weight, out_weight):
    vmem = pl.BlockSpec(memory_space=pltpu.VMEM)
    hbm = pl.BlockSpec(memory_space=pl.ANY)
    cos, sin = tables()
    blocks = lambda *shape: pltpu.VMEM(shape, BF16)
    return pl.pallas_call(
        kernel,
        out_shape=jax.ShapeDtypeStruct((BLOCK, 2048), BF16),
        in_specs=[vmem, vmem, hbm, hbm, hbm, hbm, hbm, hbm],
        out_specs=vmem,
        scratch_shapes=[
            blocks(2, BLOCK, 1024),
            blocks(2048, 1024),
            blocks(2, 1024, HEAD),
            blocks(4, 1024, 512),
            blocks(2, 2, BLOCK, HEAD),
            blocks(4, 2, BLOCK, 512),
            blocks(18, 16, BLOCK, HEAD),
            blocks(18, 8, BLOCK, HEAD),
            blocks(18, 4, BLOCK, HEAD),
            blocks(18, 2, BLOCK, HEAD),
            blocks(18, 1, BLOCK, HEAD),
            pltpu.VMEM((BLOCK, HEAD), F32),
            pltpu.VMEM((BLOCK, HEAD), F32),
            blocks(2, WINDOW, BLOCK, HEAD),
            pltpu.VMEM((BLOCK, WINDOW * BLOCK), F32),
            blocks(2, 16, 16, HALF, HEAD),
            blocks(4, 1024, 512),
            blocks(4, 2, BLOCK, 512),
            pltpu.VMEM((2, 2, 1024, 512), F32),
            blocks(2, 2, 2, 8, HALF, 512),
            blocks(2, 2, 8, HALF, 512),
            blocks(2, 2, 2, 2, HALF, 512),
            blocks(2, 2, 3, HALF, 512),
            blocks(2, 2, 2, HALF, 512),
            pltpu.SemaphoreType.DMA((SEMAPHORES,)),
            pltpu.SemaphoreType.DMA((SEMAPHORES,)),
        ],
        compiler_params=pltpu.CompilerParams(
            collective_id=0, has_side_effects=True, vmem_limit_bytes=63 << 20
        ),
    )(hidden_in, segment_ids.reshape(16, BLOCK), cos, sin, q_weight, k_weight, value_weight,
      out_weight)


def solution(mesh):
    placed = (
        P("col", "row"),
        P(),
        P(("row", "col"), None),
        P(("row", "col"), None),
        P(("row", "col"), None),
        P(("row", "col"), None),
    )
    return jax.shard_map(
        body, mesh=mesh, in_specs=placed, out_specs=P("col", "row"), check_vma=False
    )
```

time: 207 us -> 182 us (0.88)
  Pallas kernels: 205 us -> 179 us
    pallas_call x1, Pallas kernels: 205 us -> 179 us  [body(): pl.pallas_call(kernel, out_shape=jax.ShapeDtypeStruct((BLOCK, 2048), BF16...]
where the time goes in v2:
time: 182 us; the launch traced here: 181 us
  Pallas kernels  179 us (98%)
  local copies, waits for them, and re-layouts  1.88 us (1%)
    pallas_call x1, Pallas kernels, body(): pl.pallas_call(kernel, out_shape=jax.ShapeDtypeStruct((BLOCK, 2048), BF16...  179 us

profile of v2, /device:TPU:0, one launch (start us, length us, event | category | flops | bytes accessed | tf_op | source)
XLA Modules:
  0.0 180.7 jit_solution(11640021100087121939)
XLA Ops:
  0.0 178.8 %shard_map.82 = bf16[128,2048]{1,0:T(8,128)(2,1)} custom-call(bf16[128,2048]{1,0:T(8,128)(2,1)} %h_ref.1, s32[16,128]{1,0:T(8,128)} %bitcast.1, f32[2048,128]{1,0:T(8,128)} %constant.4.clone.cos_ref, f32[2048,128]{1,0:T(8,128)} %constant.5.clone.sin_ref, bf16[128,16384]{1,0:T(8,128)(2,1)} %q_ref.1, bf16[128,1024]{1,0:T(8,128)(2,1)} %k_ref.1, ...), custom_call_target="tpu_custom_call" | custom-call | tf_op jit(solution)/shard_map/pallas_call | solution.py:506
  178.8 1.9 %copy.10 = bf16[128,2048]{1,0:T(8,128)(2,1)} copy(bf16[128,2048]{1,0:T(8,128)(2,1)} %shard_map.82) | data formatting | bytes 1048576

commit v3 on v2

--- a/solution.py
+++ b/solution.py
@@ -161,41 +161,43 @@
     return cos, sin
 
 
+QUERIES = {1: (0, 2), 2: (2, 2), 3: (4, 4), 4: (8, 4), 5: (12, 4)}
 ORDER = (
-    ("H","swap"), ("H","a1"), ("S",0), ("F",0,0), ("S",1), ("H","b2"), ("F",1,0),
-    ("H","f1"), ("H","f2"), ("F",0,1), ("F",1,1), ("H","b1"), ("S",2), ("H","a2"), ("P",0),
-    ("P",1), ("F",2,0), ("F",2,1), ("S",3), ("C",17,0), ("C",16,0), ("C",3,0), ("C",1,0),
-    ("C",2,0), ("C",0,0), ("F",3,0), ("F",3,1), ("C",16,1), ("C",17,1), ("P",2), ("C",16,2),
-    ("C",0,1), ("C",1,1), ("C",3,1), ("C",2,1), ("S",4), ("C",17,2), ("P",3), ("C",7,0),
-    ("C",5,0), ("F",4,1), ("F",4,0), ("S",5), ("C",2,2), ("C",4,0), ("C",1,2), ("C",6,0),
-    ("S",6), ("C",16,3), ("S",7), ("C",3,2), ("C",0,2), ("S",8), ("C",17,3), ("C",11,0),
-    ("C",9,0), ("C",2,3), ("C",10,0), ("C",8,0), ("F",5,0), ("C",7,1), ("C",5,1), ("C",6,1),
-    ("C",4,1), ("P",4), ("C",3,3), ("C",4,2), ("C",11,1), ("C",0,3), ("C",10,1), ("C",1,3),
-    ("A",0), ("C",5,2), ("C",7,2), ("C",9,1), ("C",8,1), ("C",6,2), ("C",12,0), ("C",13,0),
-    ("C",15,0), ("G",3,0,0), ("C",14,0), ("G",3,0,1), ("C",10,2), ("C",11,2), ("G",2,0,0),
-    ("G",1,0,1), ("C",4,3), ("G",0,0,1), ("G",1,0,0), ("C",7,3), ("C",5,3), ("G",0,0,0),
-    ("C",9,2), ("C",6,3), ("G",2,0,1), ("A",1), ("C",8,2), ("G",2,1,0), ("C",14,1),
-    ("G",1,1,1), ("C",15,1), ("C",13,1), ("G",3,1,1), ("C",10,3), ("C",12,1), ("G",3,1,0),
-    ("G",2,1,1), ("G",5,0,0), ("G",0,1,1), ("G",0,1,0), ("G",4,0,1), ("C",9,3), ("G",1,1,0),
-    ("G",4,0,0), ("C",11,3), ("C",8,3), ("G",6,0,0), ("G",7,0,1), ("A",2), ("G",5,0,1),
-    ("G",4,1,1), ("C",13,2), ("C",12,2), ("G",0,2,0), ("C",15,2), ("C",14,2), ("G",3,2,1),
-    ("F",7,0), ("G",1,2,0), ("G",6,1,0), ("G",2,2,1), ("F",8,0), ("G",3,2,0), ("G",9,0,1),
-    ("G",8,0,1), ("F",5,1), ("G",10,0,1), ("G",11,0,1), ("G",6,0,1), ("G",7,0,0),
-    ("G",5,1,1), ("G",2,2,0), ("C",13,3), ("G",0,2,1), ("C",15,3), ("C",12,3), ("G",7,1,1),
-    ("G",1,2,1), ("C",14,3), ("A",3), ("G",6,1,1), ("F",7,1), ("G",11,0,0), ("G",10,0,0),
-    ("G",5,1,0), ("G",11,1,1), ("G",10,1,1), ("G",8,1,1), ("F",8,1), ("G",8,0,0),
-    ("G",4,1,0), ("F",6,1), ("G",9,0,0), ("G",7,1,0), ("F",6,0), ("G",9,1,1), ("G",13,0,1),
-    ("G",12,0,1), ("G",14,0,1), ("G",15,0,1), ("G",14,0,0), ("G",5,2,1), ("G",7,2,1),
-    ("G",4,2,1), ("G",15,0,0), ("G",6,2,1), ("O",0,1), ("G",14,1,1), ("G",12,1,1),
-    ("G",11,2,1), ("G",13,1,1), ("G",12,0,0), ("G",15,1,1), ("G",8,2,1), ("G",10,2,1),
-    ("G",13,0,0), ("G",9,2,1), ("O",0,0), ("G",13,2,1), ("G",14,2,1), ("G",12,2,1),
-    ("G",15,2,1), ("G",14,1,0), ("O",1,1), ("G",11,1,0), ("G",10,1,0), ("G",15,1,0),
-    ("G",8,1,0), ("G",7,2,0), ("G",4,2,0), ("G",12,1,0), ("G",9,1,0), ("G",13,1,0),
-    ("O",2,1), ("G",5,2,0), ("G",6,2,0), ("L",1,0), ("G",9,2,0), ("L",1,1), ("G",10,2,0),
-    ("G",11,2,0), ("G",14,2,0), ("G",8,2,0), ("G",13,2,0), ("G",12,2,0), ("G",15,2,0),
-    ("U",0,1,0), ("O",1,0), ("U",0,1,1), ("O",2,0), ("U",1,1,0), ("L",0,1), ("L",0,0),
-    ("U",1,1,1), ("U",0,0,1), ("U",0,0,0), ("U",1,0,1), ("U",2,1,1), ("U",1,0,0),
-    ("U",2,1,0), ("U",2,0,1), ("U",2,0,0),
+    ("S",1), ("H","b1"), ("H","swap"), ("H","a1"), ("F",1,0), ("S",0), ("H","b2"),
+    ("F",1,1), ("S",2), ("H","a2"), ("F",0,0), ("H","f1"), ("F",0,1), ("H","f2"), ("F",2,1),
+    ("F",2,0), ("P",1), ("S",3), ("P",0), ("P",2), ("F",3,0), ("F",3,1), ("C",0,0), ("S",4),
+    ("C",17,0), ("C",16,0), ("C",1,0), ("C",3,0), ("P",3), ("C",16,1), ("C",2,0), ("C",3,1),
+    ("C",17,1), ("F",4,1), ("C",1,1), ("F",4,0), ("S",5), ("C",4,0), ("C",0,1), ("C",7,0),
+    ("C",3,2), ("C",6,0), ("C",17,2), ("C",5,0), ("C",16,2), ("F",5,0), ("F",5,1),
+    ("C",2,1), ("P",4), ("C",0,2), ("C",1,2), ("C",6,1), ("C",2,2), ("C",7,1), ("C",4,1),
+    ("C",3,3), ("C",17,3), ("S",6), ("C",16,3), ("C",5,1), ("S",7), ("P",5), ("S",8),
+    ("C",0,3), ("C",6,2), ("F",6,1), ("C",9,0), ("C",8,0), ("C",4,2), ("C",7,2), ("C",11,0),
+    ("C",1,3), ("F",6,0), ("C",5,2), ("C",2,3), ("A",0), ("C",10,0), ("C",14,0), ("F",7,0),
+    ("F",7,1), ("C",13,0), ("C",12,0), ("C",6,3), ("C",15,0), ("S",9), ("G",0,0,1),
+    ("C",4,3), ("C",9,1), ("C",11,1), ("C",7,3), ("G",0,0,0), ("G",3,0,0), ("C",5,3),
+    ("C",8,1), ("G",2,0,0), ("G",3,0,1), ("G",1,0,1), ("G",2,0,1), ("C",10,1), ("A",1),
+    ("C",13,1), ("C",15,1), ("C",14,1), ("C",12,1), ("C",9,2), ("G",1,0,0), ("C",8,2),
+    ("C",11,2), ("C",10,2), ("F",8,0), ("G",4,0,1), ("G",6,0,0), ("G",7,0,0), ("G",5,0,0),
+    ("G",7,0,1), ("G",5,0,1), ("G",2,1,1), ("G",0,1,1), ("G",6,0,1), ("G",4,0,0),
+    ("G",3,1,0), ("G",1,1,1), ("G",0,1,0), ("G",2,1,0), ("C",13,2), ("C",14,2), ("C",15,2),
+    ("G",1,1,0), ("C",12,2), ("G",3,1,1), ("C",10,3), ("C",11,3), ("C",9,3), ("G",6,1,0),
+    ("C",8,3), ("G",4,1,1), ("G",7,1,0), ("G",6,1,1), ("G",7,1,1), ("G",5,1,1), ("G",4,1,0),
+    ("G",5,1,0), ("A",2), ("G",1,2,1), ("C",12,3), ("G",3,2,1), ("C",13,3), ("G",2,2,1),
+    ("C",15,3), ("G",0,2,1), ("C",14,3), ("A",3), ("G",11,0,1), ("G",10,0,1), ("G",9,0,1),
+    ("G",8,0,1), ("G",11,0,0), ("G",5,2,1), ("G",4,2,1), ("G",6,2,1), ("G",7,2,1),
+    ("F",9,0), ("G",12,0,1), ("G",14,0,1), ("G",15,0,1), ("F",9,1), ("G",12,0,0),
+    ("G",13,0,1), ("G",11,1,1), ("G",14,0,0), ("G",10,0,0), ("G",8,1,1), ("G",13,0,0),
+    ("G",8,0,0), ("G",11,1,0), ("G",9,1,1), ("G",15,0,0), ("G",9,0,0), ("G",10,1,1),
+    ("O",0,1), ("G",14,1,1), ("G",13,1,1), ("F",8,1), ("G",12,1,1), ("G",15,1,1),
+    ("G",11,2,1), ("G",13,1,0), ("G",12,1,0), ("G",8,2,1), ("G",10,2,1), ("G",14,1,0),
+    ("G",9,2,1), ("G",13,2,1), ("G",12,2,1), ("G",8,1,0), ("G",15,1,0), ("G",15,2,1),
+    ("G",10,1,0), ("G",0,2,0), ("G",14,2,1), ("G",3,2,0), ("G",4,2,0), ("G",9,1,0),
+    ("G",1,2,0), ("G",5,2,0), ("G",7,2,0), ("G",2,2,0), ("G",6,2,0), ("O",1,1), ("O",2,1),
+    ("L",1,1), ("L",1,0), ("G",11,2,0), ("G",10,2,0), ("G",8,2,0), ("G",15,2,0),
+    ("G",14,2,0), ("G",9,2,0), ("G",13,2,0), ("G",12,2,0), ("O",0,0), ("U",0,1,1),
+    ("U",0,1,0), ("O",1,0), ("O",2,0), ("L",0,1), ("U",1,1,1), ("L",0,0), ("U",1,1,0),
+    ("U",0,0,1), ("U",0,0,0), ("U",1,0,1), ("U",2,1,0), ("U",1,0,0), ("U",2,1,1),
+    ("U",2,0,1), ("U",2,0,0),
 )
 
 
@@ -232,15 +234,10 @@
         block = xs.at[rows(4 * y + 2 * zh + p.c)]
         flying[key] = net.remote(block, block, dev)
 
-    def swap(key, y):
-        flying[key] = net.remote(hx.at[oz], xs.at[rows(p.col)], p.dev(y=y, zh=oz))
-
-    swap("swap", p.y)
+    flying["swap"] = net.remote(hx.at[oz], xs.at[rows(p.col)], p.dev(zh=oz))
     push("a1", p.y, p.zh, to_a)
     push("b1", p.y, p.zh, to_b)
     push("c1", p.y, p.zh, to_core)
-    swap("a2", p.ya)
-    swap("b2", p.yb)
     table_copies = [
         net.local(cos_ref.at[rows(p.token_block)], cos),
         net.local(sin_ref.at[rows(p.token_block)], sin),
@@ -254,6 +251,8 @@
         elif name == "b1":
             push("h2", p.yb, p.zh, to_core)
         elif name == "swap":
+            push("a2", p.y, oz, to_a)
+            push("b2", p.y, oz, to_b)
             push("c2", p.y, oz, to_core)
         elif name == "b2":
             push("f2", p.yb, oz, to_a)
@@ -271,17 +270,28 @@
 
     weights = {}
 
+    def query_weights(t):
+        first, count = QUERIES[t]
+        return first // 4, first % 4 * HEAD, count * HEAD
+
     def act_s(t):
         if t == 0:
             weights[t] = [
                 Relay(net, p, columns(k_ref, HEAD), wkv.at[0], relkv.at[0]),
                 Relay(net, p, columns(v_ref, HEAD), wkv.at[1], relkv.at[1]),
             ]
-        elif t < 5:
-            j = t - 1
-            weights[t] = [Relay(net, p, columns(q_ref, 2048, j, 512), wq.at[j], relq.at[j])]
+        elif t < 6:
+            j, at, width = query_weights(t)
+            weights[t] = [
+                Relay(
+                    net, p,
+                    columns(q_ref, 2048, QUERIES[t][0] * HEAD // width, width),
+                    wq.at[j, :, pl.ds(at, width)],
+                    relq.at[j, :, :, pl.ds(at, width)],
+                )
+            ]
         else:
-            j = t - 5
+            j = t - 6
             weights[t] = [Relay(net, p, columns(o_ref, 2048, j, 512), wo.at[j], relo.at[j])]
 
     def act_f(t, way):
@@ -308,14 +318,15 @@
     def act_p(t):
         arrive_once("c1", "c2", "h1", "h2", "h3", "h4", "h5", "h6")
         wait_weights(t)
-        slots = (16, 17) if t == 0 else range(4 * t - 4, 4 * t)
+        slots = (16, 17) if t == 0 else range(QUERIES[t][0], sum(QUERIES[t]))
 
         def step(m, carry):
             x = xs[pl.ds(pl.multiple_of(m * 512, 512), 512), :]
             if t == 0:
                 w = jnp.concatenate([wkv[0], wkv[1]], axis=1)
             else:
-                w = wq[t - 1]
+                j, at, width = query_weights(t)
+                w = wq[j, :, at : at + width]
             y = jnp.dot(x, w, preferred_element_type=F32).astype(BF16)
             n0, n1 = lax.div(m, 2), lax.rem(m, 2)
             for i in range(4):
@@ -406,7 +417,7 @@
         return jnp.concatenate(blocks, axis=0)
 
     def act_o(u, half):
-        wait_weights(5 + u)
+        wait_weights(6 + u)
         arrive(*[("g", 4 * u + s, 3, half) for s in range(4)])
 
         def step(m, carry):
@@ -425,7 +436,7 @@
     y, ya, yb, yab = p.y, p.ya, p.yb, p.yab
 
     def act_l(half, f):
-        wait_weights(8)
+        wait_weights(9)
         arrive_once(*[("g", 12 + s, 3, half) for s in range(4)])
 
         def step(m, carry):

time: 182 us -> 174 us (0.956)
  Pallas kernels: 179 us -> 171 us
    pallas_call x1, Pallas kernels: 179 us -> 171 us  [body(): pl.pallas_call(kernel, out_shape=jax.ShapeDtypeStruct((BLOCK, 2048), BF16...]
where the time goes in v3:
time: 174 us; the launch traced here: 173 us
  Pallas kernels  171 us (98%)
  local copies, waits for them, and re-layouts  1.88 us (1%)
    pallas_call x1, Pallas kernels, body(): pl.pallas_call(kernel, out_shape=jax.ShapeDtypeStruct((BLOCK, 2048), BF16...  171 us

profile of v3, /device:TPU:0, one launch (start us, length us, event | category | flops | bytes accessed | tf_op | source)
XLA Modules:
  0.0 173.4 jit_solution(16593047533788035213)
XLA Ops:
  0.0 171.5 %shard_map.82 = bf16[128,2048]{1,0:T(8,128)(2,1)} custom-call(bf16[128,2048]{1,0:T(8,128)(2,1)} %h_ref.1, s32[16,128]{1,0:T(8,128)} %bitcast.1, f32[2048,128]{1,0:T(8,128)} %constant.4.clone.cos_ref, f32[2048,128]{1,0:T(8,128)} %constant.5.clone.sin_ref, bf16[128,16384]{1,0:T(8,128)(2,1)} %q_ref.1, bf16[128,1024]{1,0:T(8,128)(2,1)} %k_ref.1, ...), custom_call_target="tpu_custom_call" | custom-call | tf_op jit(solution)/shard_map/pallas_call | solution.py:517
  171.5 1.9 %copy.10 = bf16[128,2048]{1,0:T(8,128)(2,1)} copy(bf16[128,2048]{1,0:T(8,128)(2,1)} %shard_map.82) | data formatting | bytes 1048576

commit v4 on v3

--- a/solution.py
+++ b/solution.py
@@ -10,7 +10,6 @@
 
 HEAD = 128
 BLOCK = 128
-HALF = 64
 THETA = 500000.0
 NEGATIVE = -1e30
 SEMAPHORES = 400
@@ -115,12 +114,16 @@
 
 class Relay:
     def __init__(self, net, p, src, dst, rel):
-        self.net, self.p, self.dst, self.rel = net, p, dst, rel
+        self.net, self.p, self.src, self.dst, self.rel = net, p, src, dst, rel
+        self.waits = []
+        self.ra = net.remote(src(2 * p.yab + p.c), rel.at[0], p.dev(y=p.ya))
+        self.rb = net.remote(src(2 * p.yab + p.oc), rel.at[1], p.dev(y=p.yb))
+
+    def start(self):
+        net, p, src = self.net, self.p, self.src
         y, c, oc = p.y, p.c, p.oc
-        mine = dst.at[rows(2 * y + c)]
-        self.ra = net.remote(src(2 * p.yab + c), rel.at[0], p.dev(y=p.ya))
-        self.rb = net.remote(src(2 * p.yab + oc), rel.at[1], p.dev(y=p.yb))
-        self.waits = [
+        mine = self.dst.at[rows(2 * y + c)]
+        self.waits += [
             net.remote(src(2 * p.ya + c), mine, p.dev(y=p.ya)),
             net.remote(src(2 * p.yb + c), mine, p.dev(y=p.yb)),
             net.remote(src(2 * p.ya + oc), mine, p.dev(y=p.ya, c=oc)),
@@ -162,54 +165,61 @@
 
 
 QUERIES = {1: (0, 2), 2: (2, 2), 3: (4, 4), 4: (8, 4), 5: (12, 4)}
+HALVES = ((0, 48), (48, 80))
+GATHER_HALVES = (0, 1)
+WHOLE_STAGES = 0
 ORDER = (
-    ("S",1), ("H","b1"), ("H","swap"), ("H","a1"), ("F",1,0), ("S",0), ("H","b2"),
-    ("F",1,1), ("S",2), ("H","a2"), ("F",0,0), ("H","f1"), ("F",0,1), ("H","f2"), ("F",2,1),
-    ("F",2,0), ("P",1), ("S",3), ("P",0), ("P",2), ("F",3,0), ("F",3,1), ("C",0,0), ("S",4),
-    ("C",17,0), ("C",16,0), ("C",1,0), ("C",3,0), ("P",3), ("C",16,1), ("C",2,0), ("C",3,1),
-    ("C",17,1), ("F",4,1), ("C",1,1), ("F",4,0), ("S",5), ("C",4,0), ("C",0,1), ("C",7,0),
-    ("C",3,2), ("C",6,0), ("C",17,2), ("C",5,0), ("C",16,2), ("F",5,0), ("F",5,1),
-    ("C",2,1), ("P",4), ("C",0,2), ("C",1,2), ("C",6,1), ("C",2,2), ("C",7,1), ("C",4,1),
-    ("C",3,3), ("C",17,3), ("S",6), ("C",16,3), ("C",5,1), ("S",7), ("P",5), ("S",8),
-    ("C",0,3), ("C",6,2), ("F",6,1), ("C",9,0), ("C",8,0), ("C",4,2), ("C",7,2), ("C",11,0),
-    ("C",1,3), ("F",6,0), ("C",5,2), ("C",2,3), ("A",0), ("C",10,0), ("C",14,0), ("F",7,0),
-    ("F",7,1), ("C",13,0), ("C",12,0), ("C",6,3), ("C",15,0), ("S",9), ("G",0,0,1),
-    ("C",4,3), ("C",9,1), ("C",11,1), ("C",7,3), ("G",0,0,0), ("G",3,0,0), ("C",5,3),
-    ("C",8,1), ("G",2,0,0), ("G",3,0,1), ("G",1,0,1), ("G",2,0,1), ("C",10,1), ("A",1),
-    ("C",13,1), ("C",15,1), ("C",14,1), ("C",12,1), ("C",9,2), ("G",1,0,0), ("C",8,2),
-    ("C",11,2), ("C",10,2), ("F",8,0), ("G",4,0,1), ("G",6,0,0), ("G",7,0,0), ("G",5,0,0),
-    ("G",7,0,1), ("G",5,0,1), ("G",2,1,1), ("G",0,1,1), ("G",6,0,1), ("G",4,0,0),
-    ("G",3,1,0), ("G",1,1,1), ("G",0,1,0), ("G",2,1,0), ("C",13,2), ("C",14,2), ("C",15,2),
-    ("G",1,1,0), ("C",12,2), ("G",3,1,1), ("C",10,3), ("C",11,3), ("C",9,3), ("G",6,1,0),
-    ("C",8,3), ("G",4,1,1), ("G",7,1,0), ("G",6,1,1), ("G",7,1,1), ("G",5,1,1), ("G",4,1,0),
-    ("G",5,1,0), ("A",2), ("G",1,2,1), ("C",12,3), ("G",3,2,1), ("C",13,3), ("G",2,2,1),
-    ("C",15,3), ("G",0,2,1), ("C",14,3), ("A",3), ("G",11,0,1), ("G",10,0,1), ("G",9,0,1),
-    ("G",8,0,1), ("G",11,0,0), ("G",5,2,1), ("G",4,2,1), ("G",6,2,1), ("G",7,2,1),
-    ("F",9,0), ("G",12,0,1), ("G",14,0,1), ("G",15,0,1), ("F",9,1), ("G",12,0,0),
-    ("G",13,0,1), ("G",11,1,1), ("G",14,0,0), ("G",10,0,0), ("G",8,1,1), ("G",13,0,0),
-    ("G",8,0,0), ("G",11,1,0), ("G",9,1,1), ("G",15,0,0), ("G",9,0,0), ("G",10,1,1),
-    ("O",0,1), ("G",14,1,1), ("G",13,1,1), ("F",8,1), ("G",12,1,1), ("G",15,1,1),
-    ("G",11,2,1), ("G",13,1,0), ("G",12,1,0), ("G",8,2,1), ("G",10,2,1), ("G",14,1,0),
-    ("G",9,2,1), ("G",13,2,1), ("G",12,2,1), ("G",8,1,0), ("G",15,1,0), ("G",15,2,1),
-    ("G",10,1,0), ("G",0,2,0), ("G",14,2,1), ("G",3,2,0), ("G",4,2,0), ("G",9,1,0),
-    ("G",1,2,0), ("G",5,2,0), ("G",7,2,0), ("G",2,2,0), ("G",6,2,0), ("O",1,1), ("O",2,1),
-    ("L",1,1), ("L",1,0), ("G",11,2,0), ("G",10,2,0), ("G",8,2,0), ("G",15,2,0),
-    ("G",14,2,0), ("G",9,2,0), ("G",13,2,0), ("G",12,2,0), ("O",0,0), ("U",0,1,1),
-    ("U",0,1,0), ("O",1,0), ("O",2,0), ("L",0,1), ("U",1,1,1), ("L",0,0), ("U",1,1,0),
-    ("U",0,0,1), ("U",0,0,0), ("U",1,0,1), ("U",2,1,0), ("U",1,0,0), ("U",2,1,1),
-    ("U",2,0,1), ("U",2,0,0),
+    ("S",1,0), ("S",0,0), ("S",2,0), ("H","b1"), ("H","swap"), ("F",0,0), ("F",0,1),
+    ("F",1,1), ("H","a1"), ("F",1,0), ("H","a2"), ("H","b2"), ("S",1,1), ("S",0,1),
+    ("H","f1"), ("F",2,1), ("H","f2"), ("S",2,1), ("F",2,0), ("S",3,0), ("P",1), ("S",3,1),
+    ("P",0), ("P",2), ("F",3,0), ("C",0,0), ("C",1,0), ("F",3,1), ("C",17,0), ("S",4,0),
+    ("C",16,0), ("S",4,1), ("C",3,0), ("P",3,0), ("C",2,0), ("C",0,1), ("F",4,1),
+    ("C",16,1), ("C",1,1), ("P",3,1), ("F",4,0), ("C",17,1), ("S",5,0), ("C",3,1),
+    ("C",1,2), ("S",5,1), ("C",4,0), ("C",0,2), ("C",16,2), ("C",5,0), ("C",2,1),
+    ("C",17,2), ("P",4,0), ("C",6,0), ("C",3,2), ("P",4,1), ("F",5,0), ("F",5,1), ("C",4,1),
+    ("S",6,0), ("S",7,0), ("C",1,3), ("S",8,0), ("S",7,1), ("C",2,2), ("C",16,3), ("C",0,3),
+    ("S",6,1), ("C",3,3), ("C",7,0), ("C",17,3), ("S",8,1), ("C",8,0), ("C",5,1), ("C",9,0),
+    ("C",6,1), ("P",5,0), ("C",10,0), ("C",7,1), ("P",5,1), ("C",2,3), ("C",4,2), ("C",6,2),
+    ("C",5,2), ("S",9,0), ("A",0), ("C",9,1), ("F",6,1), ("C",11,0), ("C",10,1), ("C",12,0),
+    ("F",7,0), ("C",7,2), ("C",13,0), ("C",5,3), ("C",6,3), ("C",14,0), ("C",8,1),
+    ("G",3,0,0), ("G",3,0,1), ("G",2,0,0), ("C",15,0), ("F",6,0), ("G",1,0,1), ("G",2,0,1),
+    ("C",4,3), ("C",11,1), ("C",7,3), ("G",0,0,1), ("A",1), ("C",13,1), ("C",10,2),
+    ("G",0,0,0), ("C",9,2), ("C",12,1), ("C",15,1), ("C",14,1), ("C",8,2), ("C",11,2),
+    ("G",4,0,0), ("G",5,0,0), ("G",0,1,1), ("F",7,1), ("G",6,0,1), ("G",5,0,1), ("G",1,0,0),
+    ("G",7,0,0), ("G",3,1,0), ("F",8,1), ("G",7,0,1), ("G",4,0,1), ("G",3,1,1), ("G",2,1,0),
+    ("G",1,1,1), ("G",0,1,0), ("C",13,2), ("C",10,3), ("C",12,2), ("G",6,0,0), ("C",9,3),
+    ("G",5,1,0), ("C",11,3), ("G",2,1,1), ("C",15,2), ("C",8,3), ("C",14,2), ("G",5,1,1),
+    ("G",6,1,1), ("G",1,1,0), ("G",4,1,1), ("G",0,2,1), ("G",4,1,0), ("A",2), ("G",3,2,1),
+    ("G",7,1,1), ("C",13,3), ("G",2,2,1), ("C",15,3), ("C",12,3), ("G",1,2,1), ("C",14,3),
+    ("A",3), ("G",10,0,1), ("G",9,0,1), ("G",4,2,1), ("G",8,0,1), ("G",9,0,0), ("G",10,0,0),
+    ("G",11,0,1), ("G",5,2,1), ("G",7,2,1), ("F",8,0), ("G",12,0,0), ("F",9,1),
+    ("G",12,0,1), ("G",13,0,1), ("S",9,1), ("G",10,1,1), ("G",6,1,0), ("G",9,1,1),
+    ("G",14,0,1), ("G",6,2,1), ("G",14,0,0), ("G",11,1,1), ("G",13,0,0), ("G",7,1,0),
+    ("G",8,0,0), ("G",15,0,1), ("G",8,1,1), ("O",0,1), ("G",12,1,1), ("G",14,1,1),
+    ("G",11,0,0), ("G",15,0,0), ("G",15,1,1), ("G",13,1,1), ("G",11,2,1), ("F",9,0),
+    ("G",8,2,1), ("G",9,2,1), ("G",10,2,1), ("O",1,1), ("G",12,2,1), ("G",13,2,1),
+    ("G",14,2,1), ("G",15,2,1), ("G",10,1,0), ("G",9,1,0), ("G",3,2,0), ("G",15,1,0),
+    ("G",8,1,0), ("G",11,1,0), ("G",13,1,0), ("G",0,2,0), ("G",12,1,0), ("G",2,2,0),
+    ("G",1,2,0), ("G",14,1,0), ("G",7,2,0), ("O",2,1), ("G",6,2,0), ("G",4,2,0),
+    ("G",5,2,0), ("L",1,0), ("G",8,2,0), ("G",12,2,0), ("L",1,1), ("G",9,2,0), ("G",13,2,0),
+    ("G",11,2,0), ("G",15,2,0), ("G",10,2,0), ("O",0,0), ("G",14,2,0), ("U",0,1,0),
+    ("O",1,0), ("U",0,1,1), ("O",2,0), ("L",0,0), ("U",1,1,0), ("L",0,1), ("U",0,0,0),
+    ("U",1,1,1), ("U",0,0,1), ("U",1,0,0), ("U",1,0,1), ("U",2,1,1), ("U",2,0,0),
+    ("U",2,1,0), ("U",2,0,1),
 )
 
 
 def kernel(
     h_ref, seg_ref, cos_ref, sin_ref, q_ref, k_ref, v_ref, o_ref,
-    out_ref,
+    out_ref, more_ref,
     hx, xs, wkv, wq, relkv, relq, part, r0, r1, r2, r3, cos, sin, kv, bias,
-    att, wo, relo, acc, po, rc, ry1, ry2, fin, send, recv,
+    att, wo, relo, acc0, acc1, po0, po1, rc0, rc1, ones0, ones1, twos0, twos1, send, recv,
 ):
     p = Place()
     net = Net(send, recv)
     recvs = (r0, r1, r2, r3)
+    acc, po, rc = (acc0, acc1), (po0, po1), (rc0, rc1)
+    ones, twos = (ones0, ones1), (twos0, twos1)
     for z in range(2):
         for yy in range(4):
             hx[z, :, yy * 256 : (yy + 1) * 256] = h_ref[
@@ -274,8 +284,11 @@
         first, count = QUERIES[t]
         return first // 4, first % 4 * HEAD, count * HEAD
 
-    def act_s(t):
-        if t == 0:
+    def act_s(t, part):
+        if part:
+            for relay in weights[t]:
+                relay.start()
+        elif t == 0:
             weights[t] = [
                 Relay(net, p, columns(k_ref, HEAD), wkv.at[0], relkv.at[0]),
                 Relay(net, p, columns(v_ref, HEAD), wkv.at[1], relkv.at[1]),
@@ -315,18 +328,22 @@
             part.at[slot, pl.ds(at, n)], recvs[k].at[slot], p.partners[o[k]]
         )
 
-    def act_p(t):
+    def act_p(t, pair=0):
         arrive_once("c1", "c2", "h1", "h2", "h3", "h4", "h5", "h6")
         wait_weights(t)
-        slots = (16, 17) if t == 0 else range(QUERIES[t][0], sum(QUERIES[t]))
+        if t == 0:
+            slots = (16, 17)
+        else:
+            slots = range(QUERIES[t][0] + 2 * pair, QUERIES[t][0] + 2 * pair + 2)
+            j, at, _ = query_weights(t)
+            at = at + 256 * pair
 
         def step(m, carry):
             x = xs[pl.ds(pl.multiple_of(m * 512, 512), 512), :]
             if t == 0:
                 w = jnp.concatenate([wkv[0], wkv[1]], axis=1)
             else:
-                j, at, width = query_weights(t)
-                w = wq[j, :, at : at + width]
+                w = wq[j, :, at : at + 256]
             y = jnp.dot(x, w, preferred_element_type=F32).astype(BF16)
             n0, n1 = lax.div(m, 2), lax.rem(m, 2)
             for i in range(4):
@@ -370,10 +387,25 @@
                     p.block_dev(p.token_block + d),
                 )
 
-    def gather(slot, i, half):
+    def gather(slot, i):
         o, k = slot_order(slot), 3 - i
-        blocks = att.at[half, slot, pl.ds(prefix(p.bits, o, k + 1), 1 << i)]
+        at = pl.ds(prefix(p.bits, o, k + 1), 1 << i)
+        if i < WHOLE_STAGES:
+            blocks = att.at[slot, at]
+            flying["g", slot, i] = net.remote(blocks, blocks, p.partners[o[k]])
+
+    def gather_half(slot, i, half):
+        o, k = slot_order(slot), 3 - i
+        at = pl.ds(prefix(p.bits, o, k + 1), 1 << i)
+        blocks = att.at[slot, at, pl.ds(*HALVES[half])]
         flying["g", slot, i, half] = net.remote(blocks, blocks, p.partners[o[k]])
+
+    def gather_on(slot, i):
+        if i < WHOLE_STAGES:
+            gather(slot, i)
+        else:
+            for half in GATHER_HALVES:
+                gather_half(slot, i, half)
 
     def act_a(u):
         arrive_once(*[("window", which, d) for which in range(2) for d in range(1, WINDOW)])
@@ -395,23 +427,25 @@
         )
         attended = (attended * (1.0 / denominator)).astype(BF16)
         for s, slot in enumerate(slots):
-            at = prefix(p.bits, order(s), 4)
-            for half in range(2):
-                low = s * BLOCK + half * HALF
-                att[half, slot, at] = attended[low : low + HALF]
-                gather(slot, 0, half)
-
-    def act_g(slot, i, half):
-        arrive(("g", slot, i, half))
-        gather(slot, i + 1, half)
+            att[slot, prefix(p.bits, order(s), 4)] = attended[s * BLOCK : (s + 1) * BLOCK]
+            gather_on(slot, 0)
+
+    def act_g(slot, i, *half):
+        arrive(("g", slot, i, *half))
+        if half:
+            gather_half(slot, i + 1, *half)
+        else:
+            gather_on(slot, i + 1)
 
     def attended_rows(u, half, m):
+        low, size = HALVES[half]
         blocks = []
         for i in range(8):
             nat = (m, i // 4, i // 2 % 2, i % 2)
             blocks.append(
                 jnp.concatenate(
-                    [att[half, 4 * u + s, place_in(order(s), nat)] for s in range(4)], axis=1
+                    [att[4 * u + s, place_in(order(s), nat), low : low + size] for s in range(4)],
+                    axis=1,
                 )
             )
         return jnp.concatenate(blocks, axis=0)
@@ -419,6 +453,7 @@
     def act_o(u, half):
         wait_weights(6 + u)
         arrive(*[("g", 4 * u + s, 3, half) for s in range(4)])
+        total, size = acc[half], HALVES[half][1]
 
         def step(m, carry):
             y = lax.dot_general(
@@ -426,9 +461,9 @@
                 preferred_element_type=F32,
             )
             for f in range(2):
-                at = (half, f, pl.ds(pl.multiple_of(m * 512, 512), 512))
+                at = (f, pl.ds(pl.multiple_of(m * 8 * size, 8 * size), 8 * size))
                 term = y[:, f * 512 : (f + 1) * 512]
-                acc[at] = term if u == 0 else acc[at] + term
+                total[at] = term if u == 0 else total[at] + term
             return carry
 
         lax.fori_loop(0, 2, step, 0)
@@ -438,24 +473,25 @@
     def act_l(half, f):
         wait_weights(9)
         arrive_once(*[("g", 12 + s, 3, half) for s in range(4)])
+        size = HALVES[half][1]
 
         def step(m, carry):
             term = lax.dot_general(
                 attended_rows(3, half, m), wo[3, f * 512 : (f + 1) * 512],
                 (((1,), (1,)), ((), ())), preferred_element_type=F32,
             )
-            total = acc[half, f, pl.ds(pl.multiple_of(m * 512, 512), 512)] + term
-            total = total.astype(BF16)
+            at = pl.ds(pl.multiple_of(m * 8 * size, 8 * size), 8 * size)
+            total = (acc[half][f, at] + term).astype(BF16)
             for i in range(8):
-                po[half, f, i % 2, 4 * m + i // 2] = total[i * HALF : (i + 1) * HALF]
+                po[half][f, i % 2, 4 * m + i // 2] = total[i * size : (i + 1) * size]
             return carry
 
         lax.fori_loop(0, 2, step, 0)
-        flying["c", half, f] = net.remote(po.at[half, f, p.oc], rc.at[half, f], to_core)
+        flying["c", half, f] = net.remote(po[half].at[f, p.oc], rc[half].at[f], to_core)
 
     def act_u(stage, half, f):
-        mine, key = po.at[half, f, p.c], ("u", stage, half, f)
-        one, two = ry1.at[half, f], ry2.at[half, f]
+        mine, key = po[half].at[f, p.c], ("u", stage, half, f)
+        one, two = ones[half].at[f], twos[half].at[f]
 
         def add(at, other):
             mine[at] = mine[at] + other
@@ -466,7 +502,7 @@
         if stage == 0:
             arrive(("c", half, f))
             for i in range(8):
-                add(i, rc[half, f, i])
+                add(i, rc[half][f, i])
             hand(2 * yab + p.zh, one.at[0, 0], to_a)
             hand(2 * yab + oz, one.at[1, 0], to_b)
             hand(2 * ya + p.zh, one.at[0, 1], to_a)
@@ -482,14 +518,14 @@
             hand(2 * y + oz, two.at[2], p.dev(zh=oz))
             add(2 * y + p.zh, one[0, 1])
             return
-        fin[half, f, p.zh] = mine[2 * y + p.zh] + two[0]
-        fin[half, f, oz] = two[1] + two[2]
-        for z in range(2):
-            for e in range(2):
-                at = (2 * f + e) * 512 + z * 256
-                out_ref[half * HALF : (half + 1) * HALF, at : at + 256] = fin[
-                    half, f, z, :, e * 256 : (e + 1) * 256
-                ]
+        low, size = HALVES[half]
+        here, there = (mine[2 * y + p.zh], two[0]), (two[1], two[2])
+        for ref, mine_part, other_part in zip((out_ref, more_ref), here, there):
+            for z in range(2):
+                part_z = jnp.where(p.zh == z, mine_part, other_part)
+                for e in range(2):
+                    at = (2 * f + e) * 512 + z * 256
+                    ref[low : low + size, at : at + 256] = part_z[:, e * 256 : (e + 1) * 256]
 
     seg_q = jnp.transpose(
         jnp.broadcast_to(seg_ref[pl.ds(p.token_block, 1), :], (BLOCK, BLOCK))
@@ -514,11 +550,12 @@
     hbm = pl.BlockSpec(memory_space=pl.ANY)
     cos, sin = tables()
     blocks = lambda *shape: pltpu.VMEM(shape, BF16)
-    return pl.pallas_call(
+    sizes = [size for _, size in HALVES]
+    one, two = pl.pallas_call(
         kernel,
-        out_shape=jax.ShapeDtypeStruct((BLOCK, 2048), BF16),
+        out_shape=(jax.ShapeDtypeStruct((BLOCK, 2048), BF16),) * 2,
         in_specs=[vmem, vmem, hbm, hbm, hbm, hbm, hbm, hbm],
-        out_specs=vmem,
+        out_specs=(vmem, vmem),
         scratch_shapes=[
             blocks(2, BLOCK, 1024),
             blocks(2048, 1024),
@@ -535,15 +572,14 @@
             pltpu.VMEM((BLOCK, HEAD), F32),
             blocks(2, WINDOW, BLOCK, HEAD),
             pltpu.VMEM((BLOCK, WINDOW * BLOCK), F32),
-            blocks(2, 16, 16, HALF, HEAD),
+            blocks(16, 16, BLOCK, HEAD),
             blocks(4, 1024, 512),
             blocks(4, 2, BLOCK, 512),
-            pltpu.VMEM((2, 2, 1024, 512), F32),
-            blocks(2, 2, 2, 8, HALF, 512),
-            blocks(2, 2, 8, HALF, 512),
-            blocks(2, 2, 2, 2, HALF, 512),
-            blocks(2, 2, 3, HALF, 512),
-            blocks(2, 2, 2, HALF, 512),
+            *[pltpu.VMEM((2, 16 * size, 512), F32) for size in sizes],
+            *[blocks(2, 2, 8, size, 512) for size in sizes],
+            *[blocks(2, 8, size, 512) for size in sizes],
+            *[blocks(2, 2, 2, size, 512) for size in sizes],
+            *[blocks(2, 3, size, 512) for size in sizes],
             pltpu.SemaphoreType.DMA((SEMAPHORES,)),
             pltpu.SemaphoreType.DMA((SEMAPHORES,)),
         ],
@@ -552,6 +588,7 @@
         ),
     )(hidden_in, segment_ids.reshape(16, BLOCK), cos, sin, q_weight, k_weight, value_weight,
       out_weight)
+    return (one.astype(F32) + two.astype(F32)).astype(BF16)
 
 
 def solution(mesh):

time: 174 us -> 173 us (level)
  other arithmetic: 0 us -> 2.12 us
  local copies, waits for them, and re-layouts: 1.88 us -> 0 us
    convert_element_type x0 -> x1, other arithmetic: none -> 2.12 us  [body(): return (one.astype(F32) + two.astype(F32)).astype(BF16)]
    unnamed x1 -> x0, local copies, waits for them, and re-layouts: 1.88 us -> none
where the time goes in v4:
time: 173 us
  Pallas kernels  170 us (98%)
  other arithmetic  2.12 us (1%)
    pallas_call x1, Pallas kernels, body(): pl.pallas_call(kernel, out_shape=(jax.ShapeDtypeStruct((BLOCK, 2048), BF1...  170 us

profile of v4, /device:TPU:0, one launch (start us, length us, event | category | flops | bytes accessed | tf_op | source)
XLA Modules:
  0.0 172.6 jit_solution(6271034559545361211)
XLA Ops:
  0.0 170.5 %shard_map.82 = (bf16[128,2048]{1,0:T(8,128)(2,1)}, bf16[128,2048]{1,0:T(8,128)(2,1)}) custom-call(bf16[128,2048]{1,0:T(8,128)(2,1)} %h_ref.1, s32[16,128]{1,0:T(8,128)} %bitcast.1, f32[2048,128]{1,0:T(8,128)} %constant.4.clone.cos_ref, f32[2048,128]{1,0:T(8,128)} %constant.5.clone.sin_ref, bf16[128,16384]{1,0:T(8,128)(2,1)} %q_ref.1, ...), custom_call_target="tpu_custom_call" | custom-call | tf_op jit(solution)/shard_map/pallas_call | solution.py:554
  170.5 2.1 %add_convert_fusion = bf16[128,2048]{1,0:T(8,128)(2,1)} fusion(bf16[128,2048]{1,0:T(8,128)(2,1)} %get-tuple-element.8, bf16[128,2048]{1,0:T(8,128)(2,1)} %get-tuple-element.7), kind=kLoop, calls=%fused_computation | loop fusion | flops 1048576 | bytes 1572864 | tf_op jit(solution)/shard_map/convert_element_type | solution.py:591

commit v5 on v4

--- a/solution.py
+++ b/solution.py
@@ -85,14 +85,14 @@
     def __init__(self, send, recv):
         self.send, self.recv, self.n, self.open = send, recv, 0, []
 
-    def remote(self, src, dst, dev):
+    def remote(self, src, dst, dev, into=None):
         i = self.n
         self.n += 1
         cp = pltpu.make_async_remote_copy(
             src, dst, self.send.at[i], self.recv.at[i], device_id=dev, device_id_type=MESH
         )
         cp.start()
-        self.open.append(cp)
+        (self.open if into is None else into).append(cp)
         return cp
 
     def local(self, src, dst):
@@ -211,9 +211,9 @@
 
 def kernel(
     h_ref, seg_ref, cos_ref, sin_ref, q_ref, k_ref, v_ref, o_ref,
-    out_ref, more_ref,
+    out_ref,
     hx, xs, wkv, wq, relkv, relq, part, r0, r1, r2, r3, cos, sin, kv, bias,
-    att, wo, relo, acc0, acc1, po0, po1, rc0, rc1, ones0, ones1, twos0, twos1, send, recv,
+    att, wo, relo, acc0, acc1, po0, po1, rc0, rc1, ones0, ones1, twos0, twos1, fin, send, recv,
 ):
     p = Place()
     net = Net(send, recv)
@@ -470,6 +470,8 @@
 
     y, ya, yb, yab = p.y, p.ya, p.yb, p.yab
 
+    late, ready, results = [], [], []
+
     def act_l(half, f):
         wait_weights(9)
         arrive_once(*[("g", 12 + s, 3, half) for s in range(4)])
@@ -487,7 +489,10 @@
             return carry
 
         lax.fori_loop(0, 2, step, 0)
-        flying["c", half, f] = net.remote(po[half].at[f, p.oc], rc[half].at[f], to_core)
+        flying["c", half, f] = net.remote(po[half].at[f, p.oc], rc[half].at[f], to_core, late)
+        ready.append((half, f))
+        if len(ready) == 4:
+            net.finish()
 
     def act_u(stage, half, f):
         mine, key = po[half].at[f, p.c], ("u", stage, half, f)
@@ -497,7 +502,9 @@
             mine[at] = mine[at] + other
 
         def hand(block, dst, dev):
-            flying["u", stage + 1, half, f, len(flying)] = net.remote(mine.at[block], dst, dev)
+            flying["u", stage + 1, half, f, len(flying)] = net.remote(
+                mine.at[block], dst, dev, late
+            )
 
         if stage == 0:
             arrive(("c", half, f))
@@ -519,13 +526,14 @@
             add(2 * y + p.zh, one[0, 1])
             return
         low, size = HALVES[half]
-        here, there = (mine[2 * y + p.zh], two[0]), (two[1], two[2])
-        for ref, mine_part, other_part in zip((out_ref, more_ref), here, there):
-            for z in range(2):
-                part_z = jnp.where(p.zh == z, mine_part, other_part)
-                for e in range(2):
-                    at = (2 * f + e) * 512 + z * 256
-                    ref[low : low + size, at : at + 256] = part_z[:, e * 256 : (e + 1) * 256]
+        here, there = mine[2 * y + p.zh] + two[0], two[1] + two[2]
+        for z in range(2):
+            part_z = jnp.where(p.zh == z, here, there)
+            for e in range(2):
+                at = (2 * f + e) * 512 + z * 256
+                fin[low : low + size, at : at + 256] = part_z[:, e * 256 : (e + 1) * 256]
+        piece = (pl.ds(low, size), pl.ds(f * 1024, 1024))
+        results.append(net.local(fin.at[piece], out_ref.at[piece]))
 
     seg_q = jnp.transpose(
         jnp.broadcast_to(seg_ref[pl.ds(p.token_block, 1), :], (BLOCK, BLOCK))
@@ -542,7 +550,10 @@
     )
     for name, *arguments in ORDER:
         actions[name](*arguments)
-    net.finish()
+    for cp in late:
+        cp.wait_send()
+    for cp in results:
+        cp.wait()
 
 
 def body(hidden_in, segment_ids, q_weight, k_weight, value_weight, out_weight):
@@ -551,11 +562,11 @@
     cos, sin = tables()
     blocks = lambda *shape: pltpu.VMEM(shape, BF16)
     sizes = [size for _, size in HALVES]
-    one, two = pl.pallas_call(
+    return pl.pallas_call(
         kernel,
-        out_shape=(jax.ShapeDtypeStruct((BLOCK, 2048), BF16),) * 2,
+        out_shape=jax.ShapeDtypeStruct((BLOCK, 2048), BF16),
         in_specs=[vmem, vmem, hbm, hbm, hbm, hbm, hbm, hbm],
-        out_specs=(vmem, vmem),
+        out_specs=hbm,
         scratch_shapes=[
             blocks(2, BLOCK, 1024),
             blocks(2048, 1024),
@@ -580,6 +591,7 @@
             *[blocks(2, 8, size, 512) for size in sizes],
             *[blocks(2, 2, 2, size, 512) for size in sizes],
             *[blocks(2, 3, size, 512) for size in sizes],
+            blocks(BLOCK, 2048),
             pltpu.SemaphoreType.DMA((SEMAPHORES,)),
             pltpu.SemaphoreType.DMA((SEMAPHORES,)),
         ],
@@ -588,7 +600,6 @@
         ),
     )(hidden_in, segment_ids.reshape(16, BLOCK), cos, sin, q_weight, k_weight, value_weight,
       out_weight)
-    return (one.astype(F32) + two.astype(F32)).astype(BF16)
 
 
 def solution(mesh):

time: 173 us -> 172 us (level)
  other arithmetic: 2.12 us -> 0 us
  local copies, waits for them, and re-layouts: 0 us -> 1.88 us
    convert_element_type x1 -> x0, other arithmetic: 2.12 us -> none  [body(): return (one.astype(F32) + two.astype(F32)).astype(BF16)]
    unnamed x0 -> x1, local copies, waits for them, and re-layouts: none -> 1.88 us
where the time goes in v5:
time: 172 us; the launch traced here: 171 us
  Pallas kernels  170 us (99%)
  local copies, waits for them, and re-layouts  1.88 us (1%)
    pallas_call x1, Pallas kernels, body(): pl.pallas_call(kernel, out_shape=jax.ShapeDtypeStruct((BLOCK, 2048), BF16...  170 us

profile of v5, /device:TPU:0, one launch (start us, length us, event | category | flops | bytes accessed | tf_op | source)
XLA Modules:
  0.0 171.5 jit_solution(15919839781037214625)
XLA Ops:
  0.0 169.6 %shard_map.82 = bf16[128,2048]{1,0:T(8,128)(2,1)} custom-call(bf16[128,2048]{1,0:T(8,128)(2,1)} %h_ref.1, s32[16,128]{1,0:T(8,128)} %bitcast.1, f32[2048,128]{1,0:T(8,128)} %constant.4.clone.cos_ref, f32[2048,128]{1,0:T(8,128)} %constant.5.clone.sin_ref, bf16[128,16384]{1,0:T(8,128)(2,1)} %q_ref.1, bf16[128,1024]{1,0:T(8,128)(2,1)} %k_ref.1, ...), custom_call_target="tpu_custom_call" | custom-call | tf_op jit(solution)/shard_map/pallas_call | solution.py:565
  169.6 1.9 %copy.10 = bf16[128,2048]{1,0:T(8,128)(2,1)} copy(bf16[128,2048]{1,0:T(8,128)(2,1)} %shard_map.82) | data formatting | bytes 1048576

commit v6 on v5

--- a/solution.py
+++ b/solution.py
@@ -169,43 +169,43 @@
 GATHER_HALVES = (0, 1)
 WHOLE_STAGES = 0
 ORDER = (
-    ("S",1,0), ("S",0,0), ("S",2,0), ("H","b1"), ("H","swap"), ("F",0,0), ("F",0,1),
-    ("F",1,1), ("H","a1"), ("F",1,0), ("H","a2"), ("H","b2"), ("S",1,1), ("S",0,1),
-    ("H","f1"), ("F",2,1), ("H","f2"), ("S",2,1), ("F",2,0), ("S",3,0), ("P",1), ("S",3,1),
-    ("P",0), ("P",2), ("F",3,0), ("C",0,0), ("C",1,0), ("F",3,1), ("C",17,0), ("S",4,0),
-    ("C",16,0), ("S",4,1), ("C",3,0), ("P",3,0), ("C",2,0), ("C",0,1), ("F",4,1),
-    ("C",16,1), ("C",1,1), ("P",3,1), ("F",4,0), ("C",17,1), ("S",5,0), ("C",3,1),
-    ("C",1,2), ("S",5,1), ("C",4,0), ("C",0,2), ("C",16,2), ("C",5,0), ("C",2,1),
-    ("C",17,2), ("P",4,0), ("C",6,0), ("C",3,2), ("P",4,1), ("F",5,0), ("F",5,1), ("C",4,1),
-    ("S",6,0), ("S",7,0), ("C",1,3), ("S",8,0), ("S",7,1), ("C",2,2), ("C",16,3), ("C",0,3),
-    ("S",6,1), ("C",3,3), ("C",7,0), ("C",17,3), ("S",8,1), ("C",8,0), ("C",5,1), ("C",9,0),
-    ("C",6,1), ("P",5,0), ("C",10,0), ("C",7,1), ("P",5,1), ("C",2,3), ("C",4,2), ("C",6,2),
-    ("C",5,2), ("S",9,0), ("A",0), ("C",9,1), ("F",6,1), ("C",11,0), ("C",10,1), ("C",12,0),
-    ("F",7,0), ("C",7,2), ("C",13,0), ("C",5,3), ("C",6,3), ("C",14,0), ("C",8,1),
-    ("G",3,0,0), ("G",3,0,1), ("G",2,0,0), ("C",15,0), ("F",6,0), ("G",1,0,1), ("G",2,0,1),
-    ("C",4,3), ("C",11,1), ("C",7,3), ("G",0,0,1), ("A",1), ("C",13,1), ("C",10,2),
-    ("G",0,0,0), ("C",9,2), ("C",12,1), ("C",15,1), ("C",14,1), ("C",8,2), ("C",11,2),
-    ("G",4,0,0), ("G",5,0,0), ("G",0,1,1), ("F",7,1), ("G",6,0,1), ("G",5,0,1), ("G",1,0,0),
-    ("G",7,0,0), ("G",3,1,0), ("F",8,1), ("G",7,0,1), ("G",4,0,1), ("G",3,1,1), ("G",2,1,0),
-    ("G",1,1,1), ("G",0,1,0), ("C",13,2), ("C",10,3), ("C",12,2), ("G",6,0,0), ("C",9,3),
-    ("G",5,1,0), ("C",11,3), ("G",2,1,1), ("C",15,2), ("C",8,3), ("C",14,2), ("G",5,1,1),
-    ("G",6,1,1), ("G",1,1,0), ("G",4,1,1), ("G",0,2,1), ("G",4,1,0), ("A",2), ("G",3,2,1),
-    ("G",7,1,1), ("C",13,3), ("G",2,2,1), ("C",15,3), ("C",12,3), ("G",1,2,1), ("C",14,3),
-    ("A",3), ("G",10,0,1), ("G",9,0,1), ("G",4,2,1), ("G",8,0,1), ("G",9,0,0), ("G",10,0,0),
-    ("G",11,0,1), ("G",5,2,1), ("G",7,2,1), ("F",8,0), ("G",12,0,0), ("F",9,1),
-    ("G",12,0,1), ("G",13,0,1), ("S",9,1), ("G",10,1,1), ("G",6,1,0), ("G",9,1,1),
-    ("G",14,0,1), ("G",6,2,1), ("G",14,0,0), ("G",11,1,1), ("G",13,0,0), ("G",7,1,0),
-    ("G",8,0,0), ("G",15,0,1), ("G",8,1,1), ("O",0,1), ("G",12,1,1), ("G",14,1,1),
-    ("G",11,0,0), ("G",15,0,0), ("G",15,1,1), ("G",13,1,1), ("G",11,2,1), ("F",9,0),
-    ("G",8,2,1), ("G",9,2,1), ("G",10,2,1), ("O",1,1), ("G",12,2,1), ("G",13,2,1),
-    ("G",14,2,1), ("G",15,2,1), ("G",10,1,0), ("G",9,1,0), ("G",3,2,0), ("G",15,1,0),
-    ("G",8,1,0), ("G",11,1,0), ("G",13,1,0), ("G",0,2,0), ("G",12,1,0), ("G",2,2,0),
-    ("G",1,2,0), ("G",14,1,0), ("G",7,2,0), ("O",2,1), ("G",6,2,0), ("G",4,2,0),
-    ("G",5,2,0), ("L",1,0), ("G",8,2,0), ("G",12,2,0), ("L",1,1), ("G",9,2,0), ("G",13,2,0),
-    ("G",11,2,0), ("G",15,2,0), ("G",10,2,0), ("O",0,0), ("G",14,2,0), ("U",0,1,0),
-    ("O",1,0), ("U",0,1,1), ("O",2,0), ("L",0,0), ("U",1,1,0), ("L",0,1), ("U",0,0,0),
-    ("U",1,1,1), ("U",0,0,1), ("U",1,0,0), ("U",1,0,1), ("U",2,1,1), ("U",2,0,0),
-    ("U",2,1,0), ("U",2,0,1),
+    ("S",1,0), ("S",0,0), ("S",2,0), ("H","swap"), ("H","a1"), ("F",0,1), ("F",1,1),
+    ("F",1,0), ("F",0,0), ("H","b2"), ("H","b1"), ("S",1,1), ("S",0,1), ("F",2,0),
+    ("F",2,1), ("H","a2"), ("S",2,1), ("S",3,0), ("S",3,1), ("H","f1"), ("H","f2"), ("P",1),
+    ("P",0), ("P",2), ("C",0,0), ("F",3,1), ("F",3,0), ("C",1,0), ("S",4,0), ("C",17,0),
+    ("C",16,0), ("C",3,0), ("C",0,1), ("S",4,1), ("C",2,0), ("P",3,0), ("P",3,1),
+    ("C",17,1), ("C",16,1), ("C",2,1), ("C",3,1), ("F",4,1), ("F",4,0), ("S",5,0),
+    ("C",1,1), ("S",5,1), ("C",0,2), ("C",4,0), ("C",5,0), ("C",6,0), ("C",7,0), ("C",17,2),
+    ("C",3,2), ("P",4,0), ("C",16,2), ("P",4,1), ("C",5,1), ("F",5,1), ("F",5,0), ("S",6,0),
+    ("C",7,1), ("S",7,0), ("C",17,3), ("S",8,0), ("C",2,2), ("C",3,3), ("C",1,2), ("S",9,0),
+    ("S",6,1), ("C",6,1), ("C",4,1), ("C",0,3), ("C",16,3), ("C",8,0), ("C",9,0), ("C",7,2),
+    ("C",10,0), ("C",11,0), ("P",5,0), ("C",4,2), ("P",5,1), ("C",1,3), ("F",6,1),
+    ("S",8,1), ("C",2,3), ("C",6,2), ("F",6,0), ("A",0), ("C",7,3), ("C",9,1), ("C",5,2),
+    ("F",7,0), ("C",10,1), ("C",11,1), ("C",8,1), ("C",4,3), ("F",7,1), ("C",13,0),
+    ("F",8,1), ("C",12,0), ("F",8,0), ("G",2,0,0), ("C",6,3), ("G",1,0,0), ("F",9,1),
+    ("G",2,0,1), ("C",14,0), ("C",15,0), ("C",5,3), ("G",3,0,1), ("G",0,0,1), ("A",1),
+    ("G",1,0,1), ("C",11,2), ("G",3,0,0), ("C",9,2), ("C",8,2), ("C",10,2), ("G",0,0,0),
+    ("C",13,1), ("C",12,1), ("C",14,1), ("G",0,1,1), ("G",2,1,0), ("G",3,1,1), ("G",1,1,0),
+    ("G",4,0,1), ("G",6,0,0), ("G",5,0,0), ("C",15,1), ("G",7,0,1), ("G",6,0,1),
+    ("G",2,1,1), ("G",5,0,1), ("G",4,0,0), ("G",3,1,0), ("C",9,3), ("G",1,1,1), ("C",11,3),
+    ("C",10,3), ("G",7,0,0), ("C",8,3), ("G",0,1,0), ("A",2), ("C",12,2), ("C",13,2),
+    ("G",4,1,0), ("C",15,2), ("G",5,1,0), ("G",3,2,1), ("G",7,1,1), ("C",14,2), ("G",4,1,1),
+    ("G",5,1,1), ("G",0,2,1), ("G",8,0,0), ("G",7,1,0), ("S",7,1), ("G",9,0,0), ("G",2,2,1),
+    ("G",11,0,1), ("C",13,3), ("G",1,2,1), ("C",12,3), ("G",9,0,1), ("C",15,3), ("F",9,0),
+    ("C",14,3), ("G",6,1,1), ("A",3), ("G",10,0,1), ("G",7,2,1), ("G",8,0,1), ("G",9,1,1),
+    ("G",5,2,1), ("G",11,0,0), ("G",10,0,0), ("S",9,1), ("G",11,1,1), ("G",12,0,0),
+    ("G",15,0,1), ("G",14,0,0), ("G",14,0,1), ("G",12,0,1), ("G",13,0,1), ("G",13,0,0),
+    ("G",4,2,1), ("G",8,1,1), ("G",10,1,1), ("G",15,0,0), ("G",6,2,1), ("O",0,1),
+    ("G",14,1,1), ("G",13,1,1), ("G",12,1,1), ("G",6,1,0), ("G",15,1,1), ("G",9,2,1),
+    ("G",11,2,1), ("G",10,2,1), ("G",8,2,1), ("G",14,2,1), ("G",9,1,0), ("G",15,2,1),
+    ("G",12,2,1), ("G",15,1,0), ("G",10,1,0), ("G",13,1,0), ("G",2,2,0), ("G",14,1,0),
+    ("G",6,2,0), ("G",13,2,1), ("G",8,1,0), ("G",3,2,0), ("G",12,1,0), ("G",11,1,0),
+    ("G",1,2,0), ("G",5,2,0), ("G",0,2,0), ("O",1,1), ("G",4,2,0), ("O",2,1), ("G",7,2,0),
+    ("L",1,1), ("G",9,2,0), ("G",10,2,0), ("G",14,2,0), ("G",13,2,0), ("L",1,0),
+    ("G",8,2,0), ("G",12,2,0), ("G",11,2,0), ("O",0,0), ("G",15,2,0), ("U",0,1,1),
+    ("O",1,0), ("U",0,1,0), ("O",2,0), ("L",0,1), ("U",1,1,1), ("L",0,0), ("U",0,0,1),
+    ("U",1,1,0), ("U",0,0,0), ("U",2,1,1), ("U",1,0,1), ("U",1,0,0), ("U",2,1,0),
+    ("U",2,0,1), ("U",2,0,0),
 )
 
 

time: 172 us -> 172 us (level)
  no operation moved by 1% of the time
where the time goes in v6:
time: 172 us; the launch traced here: 171 us
  Pallas kernels  170 us (99%)
  local copies, waits for them, and re-layouts  1.88 us (1%)
    pallas_call x1, Pallas kernels, body(): pl.pallas_call(kernel, out_shape=jax.ShapeDtypeStruct((BLOCK, 2048), BF16...  170 us

profile of v6, /device:TPU:0, one launch (start us, length us, event | category | flops | bytes accessed | tf_op | source)
XLA Modules:
  0.0 171.5 jit_solution(11123224600439169401)
XLA Ops:
  0.0 169.6 %shard_map.82 = bf16[128,2048]{1,0:T(8,128)(2,1)} custom-call(bf16[128,2048]{1,0:T(8,128)(2,1)} %h_ref.1, s32[16,128]{1,0:T(8,128)} %bitcast.1, f32[2048,128]{1,0:T(8,128)} %constant.4.clone.cos_ref, f32[2048,128]{1,0:T(8,128)} %constant.5.clone.sin_ref, bf16[128,16384]{1,0:T(8,128)(2,1)} %q_ref.1, bf16[128,1024]{1,0:T(8,128)(2,1)} %k_ref.1, ...), custom_call_target="tpu_custom_call" | custom-call | tf_op jit(solution)/shard_map/pallas_call | solution.py:565
  169.6 1.9 %copy.10 = bf16[128,2048]{1,0:T(8,128)(2,1)} copy(bf16[128,2048]{1,0:T(8,128)(2,1)} %shard_map.82) | data formatting | bytes 1048576

commit v7 on v6

--- a/solution.py
+++ b/solution.py
@@ -169,50 +169,50 @@
 GATHER_HALVES = (0, 1)
 WHOLE_STAGES = 0
 ORDER = (
-    ("S",1,0), ("S",0,0), ("S",2,0), ("H","swap"), ("H","a1"), ("F",0,1), ("F",1,1),
-    ("F",1,0), ("F",0,0), ("H","b2"), ("H","b1"), ("S",1,1), ("S",0,1), ("F",2,0),
-    ("F",2,1), ("H","a2"), ("S",2,1), ("S",3,0), ("S",3,1), ("H","f1"), ("H","f2"), ("P",1),
-    ("P",0), ("P",2), ("C",0,0), ("F",3,1), ("F",3,0), ("C",1,0), ("S",4,0), ("C",17,0),
-    ("C",16,0), ("C",3,0), ("C",0,1), ("S",4,1), ("C",2,0), ("P",3,0), ("P",3,1),
-    ("C",17,1), ("C",16,1), ("C",2,1), ("C",3,1), ("F",4,1), ("F",4,0), ("S",5,0),
-    ("C",1,1), ("S",5,1), ("C",0,2), ("C",4,0), ("C",5,0), ("C",6,0), ("C",7,0), ("C",17,2),
-    ("C",3,2), ("P",4,0), ("C",16,2), ("P",4,1), ("C",5,1), ("F",5,1), ("F",5,0), ("S",6,0),
-    ("C",7,1), ("S",7,0), ("C",17,3), ("S",8,0), ("C",2,2), ("C",3,3), ("C",1,2), ("S",9,0),
-    ("S",6,1), ("C",6,1), ("C",4,1), ("C",0,3), ("C",16,3), ("C",8,0), ("C",9,0), ("C",7,2),
-    ("C",10,0), ("C",11,0), ("P",5,0), ("C",4,2), ("P",5,1), ("C",1,3), ("F",6,1),
-    ("S",8,1), ("C",2,3), ("C",6,2), ("F",6,0), ("A",0), ("C",7,3), ("C",9,1), ("C",5,2),
-    ("F",7,0), ("C",10,1), ("C",11,1), ("C",8,1), ("C",4,3), ("F",7,1), ("C",13,0),
-    ("F",8,1), ("C",12,0), ("F",8,0), ("G",2,0,0), ("C",6,3), ("G",1,0,0), ("F",9,1),
-    ("G",2,0,1), ("C",14,0), ("C",15,0), ("C",5,3), ("G",3,0,1), ("G",0,0,1), ("A",1),
-    ("G",1,0,1), ("C",11,2), ("G",3,0,0), ("C",9,2), ("C",8,2), ("C",10,2), ("G",0,0,0),
-    ("C",13,1), ("C",12,1), ("C",14,1), ("G",0,1,1), ("G",2,1,0), ("G",3,1,1), ("G",1,1,0),
-    ("G",4,0,1), ("G",6,0,0), ("G",5,0,0), ("C",15,1), ("G",7,0,1), ("G",6,0,1),
-    ("G",2,1,1), ("G",5,0,1), ("G",4,0,0), ("G",3,1,0), ("C",9,3), ("G",1,1,1), ("C",11,3),
-    ("C",10,3), ("G",7,0,0), ("C",8,3), ("G",0,1,0), ("A",2), ("C",12,2), ("C",13,2),
-    ("G",4,1,0), ("C",15,2), ("G",5,1,0), ("G",3,2,1), ("G",7,1,1), ("C",14,2), ("G",4,1,1),
-    ("G",5,1,1), ("G",0,2,1), ("G",8,0,0), ("G",7,1,0), ("S",7,1), ("G",9,0,0), ("G",2,2,1),
-    ("G",11,0,1), ("C",13,3), ("G",1,2,1), ("C",12,3), ("G",9,0,1), ("C",15,3), ("F",9,0),
-    ("C",14,3), ("G",6,1,1), ("A",3), ("G",10,0,1), ("G",7,2,1), ("G",8,0,1), ("G",9,1,1),
-    ("G",5,2,1), ("G",11,0,0), ("G",10,0,0), ("S",9,1), ("G",11,1,1), ("G",12,0,0),
-    ("G",15,0,1), ("G",14,0,0), ("G",14,0,1), ("G",12,0,1), ("G",13,0,1), ("G",13,0,0),
-    ("G",4,2,1), ("G",8,1,1), ("G",10,1,1), ("G",15,0,0), ("G",6,2,1), ("O",0,1),
-    ("G",14,1,1), ("G",13,1,1), ("G",12,1,1), ("G",6,1,0), ("G",15,1,1), ("G",9,2,1),
-    ("G",11,2,1), ("G",10,2,1), ("G",8,2,1), ("G",14,2,1), ("G",9,1,0), ("G",15,2,1),
-    ("G",12,2,1), ("G",15,1,0), ("G",10,1,0), ("G",13,1,0), ("G",2,2,0), ("G",14,1,0),
-    ("G",6,2,0), ("G",13,2,1), ("G",8,1,0), ("G",3,2,0), ("G",12,1,0), ("G",11,1,0),
-    ("G",1,2,0), ("G",5,2,0), ("G",0,2,0), ("O",1,1), ("G",4,2,0), ("O",2,1), ("G",7,2,0),
-    ("L",1,1), ("G",9,2,0), ("G",10,2,0), ("G",14,2,0), ("G",13,2,0), ("L",1,0),
-    ("G",8,2,0), ("G",12,2,0), ("G",11,2,0), ("O",0,0), ("G",15,2,0), ("U",0,1,1),
-    ("O",1,0), ("U",0,1,0), ("O",2,0), ("L",0,1), ("U",1,1,1), ("L",0,0), ("U",0,0,1),
-    ("U",1,1,0), ("U",0,0,0), ("U",2,1,1), ("U",1,0,1), ("U",1,0,0), ("U",2,1,0),
-    ("U",2,0,1), ("U",2,0,0),
+    ("S",1,0), ("S",0,0), ("S",2,0), ("H","z0"), ("H","z1"), ("H","swap"), ("H","a1"),
+    ("F",0,1), ("F",1,1), ("F",1,0), ("F",0,0), ("H","b2"), ("H","b1"), ("S",1,1),
+    ("S",0,1), ("F",2,0), ("F",2,1), ("H","a2"), ("S",2,1), ("S",3,0), ("S",3,1),
+    ("H","f1"), ("H","f2"), ("P",1), ("P",0), ("P",2), ("C",0,0), ("F",3,1), ("F",3,0),
+    ("C",1,0), ("S",4,0), ("C",17,0), ("C",16,0), ("C",3,0), ("C",0,1), ("S",4,1),
+    ("C",2,0), ("P",3,0), ("P",3,1), ("C",17,1), ("C",16,1), ("C",2,1), ("C",3,1),
+    ("F",4,1), ("F",4,0), ("S",5,0), ("C",1,1), ("S",5,1), ("C",0,2), ("C",4,0), ("C",5,0),
+    ("C",6,0), ("C",7,0), ("C",17,2), ("C",3,2), ("P",4,0), ("C",16,2), ("P",4,1),
+    ("C",5,1), ("F",5,1), ("F",5,0), ("S",6,0), ("C",7,1), ("S",7,0), ("C",17,3), ("S",8,0),
+    ("C",2,2), ("C",3,3), ("C",1,2), ("S",9,0), ("S",6,1), ("C",6,1), ("C",4,1), ("C",0,3),
+    ("C",16,3), ("C",8,0), ("C",9,0), ("C",7,2), ("C",10,0), ("C",11,0), ("P",5,0),
+    ("C",4,2), ("P",5,1), ("C",1,3), ("F",6,1), ("S",8,1), ("C",2,3), ("C",6,2), ("F",6,0),
+    ("A",0), ("C",7,3), ("C",9,1), ("C",5,2), ("F",7,0), ("C",10,1), ("C",11,1), ("C",8,1),
+    ("C",4,3), ("F",7,1), ("C",13,0), ("F",8,1), ("C",12,0), ("F",8,0), ("G",2,0,0),
+    ("C",6,3), ("G",1,0,0), ("F",9,1), ("G",2,0,1), ("C",14,0), ("C",15,0), ("C",5,3),
+    ("G",3,0,1), ("G",0,0,1), ("A",1), ("G",1,0,1), ("C",11,2), ("G",3,0,0), ("C",9,2),
+    ("C",8,2), ("C",10,2), ("G",0,0,0), ("C",13,1), ("C",12,1), ("C",14,1), ("G",0,1,1),
+    ("G",2,1,0), ("G",3,1,1), ("G",1,1,0), ("G",4,0,1), ("G",6,0,0), ("G",5,0,0),
+    ("C",15,1), ("G",7,0,1), ("G",6,0,1), ("G",2,1,1), ("G",5,0,1), ("G",4,0,0),
+    ("G",3,1,0), ("C",9,3), ("G",1,1,1), ("C",11,3), ("C",10,3), ("G",7,0,0), ("C",8,3),
+    ("G",0,1,0), ("A",2), ("C",12,2), ("C",13,2), ("G",4,1,0), ("C",15,2), ("G",5,1,0),
+    ("G",3,2,1), ("G",7,1,1), ("C",14,2), ("G",4,1,1), ("G",5,1,1), ("G",0,2,1),
+    ("G",8,0,0), ("G",7,1,0), ("S",7,1), ("G",9,0,0), ("G",2,2,1), ("G",11,0,1), ("C",13,3),
+    ("G",1,2,1), ("C",12,3), ("G",9,0,1), ("C",15,3), ("F",9,0), ("C",14,3), ("G",6,1,1),
+    ("A",3), ("G",10,0,1), ("G",7,2,1), ("G",8,0,1), ("G",9,1,1), ("G",5,2,1), ("G",11,0,0),
+    ("G",10,0,0), ("S",9,1), ("G",11,1,1), ("G",12,0,0), ("G",15,0,1), ("G",14,0,0),
+    ("G",14,0,1), ("G",12,0,1), ("G",13,0,1), ("G",13,0,0), ("G",4,2,1), ("G",8,1,1),
+    ("G",10,1,1), ("G",15,0,0), ("G",6,2,1), ("O",0,1), ("G",14,1,1), ("G",13,1,1),
+    ("G",12,1,1), ("G",6,1,0), ("G",15,1,1), ("G",9,2,1), ("G",11,2,1), ("G",10,2,1),
+    ("G",8,2,1), ("G",14,2,1), ("G",9,1,0), ("G",15,2,1), ("G",12,2,1), ("G",15,1,0),
+    ("G",10,1,0), ("G",13,1,0), ("G",2,2,0), ("G",14,1,0), ("G",6,2,0), ("G",13,2,1),
+    ("G",8,1,0), ("G",3,2,0), ("G",12,1,0), ("G",11,1,0), ("G",1,2,0), ("G",5,2,0),
+    ("G",0,2,0), ("O",1,1), ("G",4,2,0), ("O",2,1), ("G",7,2,0), ("L",1,1), ("G",9,2,0),
+    ("G",10,2,0), ("G",14,2,0), ("G",13,2,0), ("L",1,0), ("G",8,2,0), ("G",12,2,0),
+    ("G",11,2,0), ("O",0,0), ("G",15,2,0), ("U",0,1,1), ("O",1,0), ("U",0,1,0), ("O",2,0),
+    ("L",0,1), ("U",1,1,1), ("L",0,0), ("U",0,0,1), ("U",1,1,0), ("U",0,0,0), ("U",2,1,1),
+    ("U",1,0,1), ("U",1,0,0), ("U",2,1,0), ("U",2,0,1), ("U",2,0,0),
 )
 
 
 def kernel(
     h_ref, seg_ref, cos_ref, sin_ref, q_ref, k_ref, v_ref, o_ref,
     out_ref,
-    hx, xs, wkv, wq, relkv, relq, part, r0, r1, r2, r3, cos, sin, kv, bias,
+    hx, hop, xs, wkv, wq, relkv, relq, part, r0, r1, r2, r3, cos, sin, kv, bias,
     att, wo, relo, acc0, acc1, po0, po1, rc0, rc1, ones0, ones1, twos0, twos1, fin, send, recv,
 ):
     p = Place()
@@ -244,7 +244,9 @@
         block = xs.at[rows(4 * y + 2 * zh + p.c)]
         flying[key] = net.remote(block, block, dev)
 
-    flying["swap"] = net.remote(hx.at[oz], xs.at[rows(p.col)], p.dev(zh=oz))
+    (to_zb, to_za), low, high = p.partners[2:], pl.ds(0, 64), pl.ds(64, 64)
+    flying["z0"] = net.remote(hx.at[oz, low], hop.at[0], to_za)
+    flying["z1"] = net.remote(hx.at[oz, high], hop.at[1], to_zb)
     push("a1", p.y, p.zh, to_a)
     push("b1", p.y, p.zh, to_b)
     push("c1", p.y, p.zh, to_core)
@@ -253,9 +255,19 @@
         net.local(sin_ref.at[rows(p.token_block)], sin),
     ]
 
+    def half_rows(zh, first):
+        return xs.at[pl.ds(pl.multiple_of((4 * p.y + 2 * zh + p.c) * BLOCK + first, 64), 64)]
+
     def act_h(name):
-        arrive(name)
-        if name == "a1":
+        if name == "swap":
+            arrive("swap0", "swap1")
+        else:
+            arrive(name)
+        if name == "z0":
+            flying["swap0"] = net.remote(hop.at[0], half_rows(p.zh, 0), to_zb)
+        elif name == "z1":
+            flying["swap1"] = net.remote(hop.at[1], half_rows(oz, 64), to_za)
+        elif name == "a1":
             push("f1", p.ya, p.zh, to_b)
             push("h1", p.ya, p.zh, to_core)
         elif name == "b1":
@@ -339,22 +351,21 @@
             at = at + 256 * pair
 
         def step(m, carry):
-            x = xs[pl.ds(pl.multiple_of(m * 512, 512), 512), :]
+            x = xs[pl.ds(pl.multiple_of(m * 1024, 1024), 1024), :]
             if t == 0:
                 w = jnp.concatenate([wkv[0], wkv[1]], axis=1)
             else:
                 w = wq[j, :, at : at + 256]
             y = jnp.dot(x, w, preferred_element_type=F32).astype(BF16)
-            n0, n1 = lax.div(m, 2), lax.rem(m, 2)
-            for i in range(4):
-                nat = (n0, n1, i // 2, i % 2)
+            for i in range(8):
+                nat = (m, i // 4, i // 2 % 2, i % 2)
                 for g, slot in enumerate(slots):
                     part[slot, place_in(slot_order(slot), nat)] = y[
                         i * BLOCK : (i + 1) * BLOCK, g * HEAD : (g + 1) * HEAD
                     ]
             return carry
 
-        lax.fori_loop(0, 4, step, 0)
+        lax.fori_loop(0, 2, step, 0)
         for slot in slots:
             scatter(slot, 0)
 
@@ -437,11 +448,11 @@
         else:
             gather_on(slot, i + 1)
 
-    def attended_rows(u, half, m):
+    def attended_rows(u, half):
         low, size = HALVES[half]
         blocks = []
-        for i in range(8):
-            nat = (m, i // 4, i // 2 % 2, i % 2)
+        for i in range(16):
+            nat = (i // 8, i // 4 % 2, i // 2 % 2, i % 2)
             blocks.append(
                 jnp.concatenate(
                     [att[4 * u + s, place_in(order(s), nat), low : low + size] for s in range(4)],
@@ -453,17 +464,14 @@
     def act_o(u, half):
         wait_weights(6 + u)
         arrive(*[("g", 4 * u + s, 3, half) for s in range(4)])
-        total, size = acc[half], HALVES[half][1]
-
-        def step(m, carry):
-            y = lax.dot_general(
-                attended_rows(u, half, m), wo[u], (((1,), (1,)), ((), ())),
+        total = acc[half]
+
+        def step(f, carry):
+            term = lax.dot_general(
+                attended_rows(u, half), wo[u, rows(4 * f, 4)], (((1,), (1,)), ((), ())),
                 preferred_element_type=F32,
             )
-            for f in range(2):
-                at = (f, pl.ds(pl.multiple_of(m * 8 * size, 8 * size), 8 * size))
-                term = y[:, f * 512 : (f + 1) * 512]
-                total[at] = term if u == 0 else total[at] + term
+            total[f] = term if u == 0 else total[f] + term
             return carry
 
         lax.fori_loop(0, 2, step, 0)
@@ -477,18 +485,13 @@
         arrive_once(*[("g", 12 + s, 3, half) for s in range(4)])
         size = HALVES[half][1]
 
-        def step(m, carry):
-            term = lax.dot_general(
-                attended_rows(3, half, m), wo[3, f * 512 : (f + 1) * 512],
-                (((1,), (1,)), ((), ())), preferred_element_type=F32,
-            )
-            at = pl.ds(pl.multiple_of(m * 8 * size, 8 * size), 8 * size)
-            total = (acc[half][f, at] + term).astype(BF16)
-            for i in range(8):
-                po[half][f, i % 2, 4 * m + i // 2] = total[i * size : (i + 1) * size]
-            return carry
-
-        lax.fori_loop(0, 2, step, 0)
+        term = lax.dot_general(
+            attended_rows(3, half), wo[3, f * 512 : (f + 1) * 512], (((1,), (1,)), ((), ())),
+            preferred_element_type=F32,
+        )
+        total = (acc[half][f] + term).astype(BF16)
+        for i in range(16):
+            po[half][f, i % 2, i // 2] = total[i * size : (i + 1) * size]
         flying["c", half, f] = net.remote(po[half].at[f, p.oc], rc[half].at[f], to_core, late)
         ready.append((half, f))
         if len(ready) == 4:
@@ -569,6 +572,7 @@
         out_specs=hbm,
         scratch_shapes=[
             blocks(2, BLOCK, 1024),
+            blocks(2, 64, 1024),
             blocks(2048, 1024),
             blocks(2, 1024, HEAD),
             blocks(4, 1024, 512),

time: 172 us -> 171 us (level)
  no operation moved by 1% of the time
where the time goes in v7:
time: 171 us
  Pallas kernels  169 us (99%)
  local copies, waits for them, and re-layouts  1.88 us (1%)
    pallas_call x1, Pallas kernels, body(): pl.pallas_call(kernel, out_shape=jax.ShapeDtypeStruct((BLOCK, 2048), BF16...  169 us

profile of v7, /device:TPU:0, one launch (start us, length us, event | category | flops | bytes accessed | tf_op | source)
XLA Modules:
  0.0 170.6 jit_solution(15159274825422949854)
XLA Ops:
  0.0 168.7 %shard_map.82 = bf16[128,2048]{1,0:T(8,128)(2,1)} custom-call(bf16[128,2048]{1,0:T(8,128)(2,1)} %h_ref.1, s32[16,128]{1,0:T(8,128)} %bitcast.1, f32[2048,128]{1,0:T(8,128)} %constant.4.clone.cos_ref, f32[2048,128]{1,0:T(8,128)} %constant.5.clone.sin_ref, bf16[128,16384]{1,0:T(8,128)(2,1)} %q_ref.1, bf16[128,1024]{1,0:T(8,128)(2,1)} %k_ref.1, ...), custom_call_target="tpu_custom_call" | custom-call | tf_op jit(solution)/shard_map/pallas_call | solution.py:568
  168.7 1.9 %copy.10 = bf16[128,2048]{1,0:T(8,128)(2,1)} copy(bf16[128,2048]{1,0:T(8,128)(2,1)} %shard_map.82) | data formatting | bytes 1048576

commit v8 on v7

--- a/solution.py
+++ b/solution.py
@@ -220,13 +220,14 @@
     recvs = (r0, r1, r2, r3)
     acc, po, rc = (acc0, acc1), (po0, po1), (rc0, rc1)
     ones, twos = (ones0, ones1), (twos0, twos1)
-    for z in range(2):
+    inputs = []
+    for z, dst in ((1 - p.zh, hx), (p.zh, xs.at[rows(p.col)])):
         for yy in range(4):
-            hx[z, :, yy * 256 : (yy + 1) * 256] = h_ref[
-                :, yy * 512 + z * 256 : yy * 512 + z * 256 + 256
-            ]
-    xs[rows(p.col)] = hx[p.zh]
+            at = pl.ds(pl.multiple_of(yy * 512 + z * 256, 256), 256)
+            inputs.append(net.local(h_ref.at[:, at], dst.at[:, pl.ds(yy * 256, 256)]))
     barrier(p.all_partners())
+    for cp in inputs:
+        cp.wait()
 
     flying = {}
 
@@ -245,8 +246,8 @@
         flying[key] = net.remote(block, block, dev)
 
     (to_zb, to_za), low, high = p.partners[2:], pl.ds(0, 64), pl.ds(64, 64)
-    flying["z0"] = net.remote(hx.at[oz, low], hop.at[0], to_za)
-    flying["z1"] = net.remote(hx.at[oz, high], hop.at[1], to_zb)
+    flying["z0"] = net.remote(hx.at[low], hop.at[0], to_za)
+    flying["z1"] = net.remote(hx.at[high], hop.at[1], to_zb)
     push("a1", p.y, p.zh, to_a)
     push("b1", p.y, p.zh, to_b)
     push("c1", p.y, p.zh, to_core)
@@ -568,10 +569,10 @@
     return pl.pallas_call(
         kernel,
         out_shape=jax.ShapeDtypeStruct((BLOCK, 2048), BF16),
-        in_specs=[vmem, vmem, hbm, hbm, hbm, hbm, hbm, hbm],
+        in_specs=[hbm, vmem, hbm, hbm, hbm, hbm, hbm, hbm],
         out_specs=hbm,
         scratch_shapes=[
-            blocks(2, BLOCK, 1024),
+            blocks(BLOCK, 1024),
             blocks(2, 64, 1024),
             blocks(2048, 1024),
             blocks(2, 1024, HEAD),

time: 171 us -> 171 us (level)
  no operation moved by 1% of the time
where the time goes in v8:
time: 171 us; the launch traced here: 170 us
  Pallas kernels  168 us (98%)
  local copies, waits for them, and re-layouts  1.88 us (1%)
    pallas_call x1, Pallas kernels, body(): pl.pallas_call(kernel, out_shape=jax.ShapeDtypeStruct((BLOCK, 2048), BF16...  168 us

profile of v8, /device:TPU:0, one launch (start us, length us, event | category | flops | bytes accessed | tf_op | source)
XLA Modules:
  0.0 170.2 jit_solution(16222347355547182081)
XLA Ops:
  0.0 168.3 %shard_map.82 = bf16[128,2048]{1,0:T(8,128)(2,1)} custom-call(bf16[128,2048]{1,0:T(8,128)(2,1)} %h_ref.1, s32[16,128]{1,0:T(8,128)} %bitcast.1, f32[2048,128]{1,0:T(8,128)} %constant.4.clone.cos_ref, f32[2048,128]{1,0:T(8,128)} %constant.5.clone.sin_ref, bf16[128,16384]{1,0:T(8,128)(2,1)} %q_ref.1, bf16[128,1024]{1,0:T(8,128)(2,1)} %k_ref.1, ...), custom_call_target="tpu_custom_call" | custom-call | tf_op jit(solution)/shard_map/pallas_call | solution.py:569
  168.3 1.9 %copy.10 = bf16[128,2048]{1,0:T(8,128)(2,1)} copy(bf16[128,2048]{1,0:T(8,128)(2,1)} %shard_map.82) | data formatting | bytes 1048576
